TPU v7x, 256 devices: a whole 4x4x8 slice. The times are simulated.
256 devices in a mesh: cols: 32 (over y, x, core), rows: 8 (over z).
Axes of the slice: x: 4, y: 4, z: 8, core: 2. Of those that a mesh axis runs over, the one named last changes fastest.
Arguments:
- panel: bfloat16 [16, 96, 1024, 128], P('rows', 'cols'), may hold values from -0.1875 to 0.1875
- row_k: bfloat16 [96, 1024, 128], P('cols', 'rows'), as said below
- mask: int32 [16, 96], P('rows', 'cols'), may hold values 0 or 1
- a_low: bfloat16 [16, 1024, 128], P('rows'), may hold values from -0.375 to 0.375
- a_diag: float32 [1024, 1024], P('rows'), as said below
- sketch: bfloat16 [1024, 64], replicated, may hold values from -6 to 6
Outputs:
- panel_out: float32 [16, 1024, 128], P('rows')
- diag_factor: float32 [1024, 1024], P('rows')
Inputs may be any that keep to these rules, and one draw needn't show every extreme that they name: row_k entries are normal with deviation 1024 ** -0.5, cut at six deviations. a_diag - update is symmetric, with every eigenvalue 2 or more.
All inputs are finite; a program needn't handle non-finite values. No bound on the sum of `mask` on one device may be relied on, other than what follows from the above.
Results may differ from a plain program's by a relative error of at most 0.02.
Values may be sent and summed in bfloat16 or wider, within the bound.
A program may use at most 128 MiB of HBM per device.

v0:
```python
import jax
import jax.numpy as jnp
from jax import lax
from jax.sharding import PartitionSpec as P


def joined_along(blocks, dim):
    blocks = jnp.moveaxis(blocks, 0, dim)
    lengths = blocks.shape
    return blocks.reshape(*lengths[:dim], lengths[dim] * lengths[dim + 1], *lengths[dim + 2 :])


def from_everyone(value, axis):
    count = lax.axis_size(axis)
    return lax.all_to_all(
        jnp.broadcast_to(value[None], (count, *value.shape)), axis, 0, 0, tiled=True
    )


def collect(value, axis, dim):
    return joined_along(from_everyone(value, axis), dim)


def split_up(value, dim, count):
    before, after = (value.shape[:dim], value.shape[dim + 1 :])
    return jnp.moveaxis(value.reshape(*before, count, -1, *after), dim, 0)


def sum_at_owner(value, axis, dim):
    count = lax.axis_size(axis)
    blocks = lax.all_to_all(split_up(value, dim, count), axis, 0, 0, tiled=True)
    return jnp.sum(blocks.astype(jnp.float32), axis=0)


def padded_to(lines, count):
    spare = -lines.shape[0] % count
    if not spare:
        return lines
    return jnp.concatenate([lines, jnp.zeros((spare, *lines.shape[1:]), lines.dtype)])


def total_of(value, axes):
    lines = value.reshape(-1, value.shape[-1])
    own = sum_at_owner(padded_to(lines, lax.axis_size(axes)), axes, 0)
    whole = collect(own.astype(jnp.bfloat16), axes, 0)
    return whole[: len(lines)].reshape(value.shape).astype(jnp.float32)


def summed_on_arrival(value, axis, dim):
    count = lax.axis_size(axis)
    blocks = lax.all_to_all(split_up(value, dim, count), axis, 0, 0, tiled=True)
    return jnp.sum(blocks, axis=0)


def apply_inverse(gram_matrix, field):
    lower_factor = jnp.linalg.cholesky(gram_matrix)
    turned = lax.linalg.triangular_solve(
        lower_factor, jnp.transpose(field, (1, 2, 0)), left_side=True, lower=True
    )
    return jnp.transpose(turned, (2, 0, 1))


def shards(panel, row_k, mask, a_low, a_diag, sketch):
    f32 = jnp.float32
    bf16 = jnp.bfloat16
    half_width = panel.shape[-1] // 2
    tile_order = panel.shape[2]
    rows_here = panel.shape[0]
    rank_cols = sketch.shape[1]
    share_count = tile_order // lax.axis_size("cols")
    share_offset = lax.axis_index("cols") * share_count

    def flatten_rows(values):
        return values.reshape(values.shape[0], rows_here * rank_cols)

    def split_rows(values):
        return values.reshape(values.shape[0], rows_here, rank_cols)

    whole_row = collect(row_k, "rows", 1)
    k_left = whole_row[..., :half_width]
    k_right = whole_row[..., half_width:]
    own_left = row_k[..., :half_width]
    diag_core = jnp.einsum("jbr,jbs->jrs", k_right, k_right, preferred_element_type=f32).astype(
        bf16
    )
    own_mixed = jnp.einsum("jbr,jrs->jbs", own_left, diag_core, preferred_element_type=f32).astype(
        bf16
    )
    diag_part = jnp.einsum("jbs,jcs->bc", own_mixed, k_left, preferred_element_type=f32)
    diag_sum = total_of(diag_part.astype(jnp.bfloat16), "cols")
    whole_diag = lax.all_gather(
        (a_diag - diag_sum).astype(jnp.bfloat16), "rows", axis=0, tiled=True
    ).astype(jnp.float32)
    factor = jnp.linalg.cholesky(whole_diag)
    slab_rows = a_diag.shape[0]
    diag_out = lax.dynamic_slice_in_dim(factor, lax.axis_index("rows") * slab_rows, slab_rows, 0)
    left_part = panel[..., :half_width]
    right_part = panel[..., half_width:]
    weights = mask.astype(f32)[:, :, None, None]
    core = (
        jnp.einsum("ijbr,jbs->ijrs", right_part, k_right, preferred_element_type=f32) * weights
    ).astype(bf16)
    mixed_left = jnp.einsum("ijbr,ijrs->ijbs", left_part, core, preferred_element_type=f32).astype(
        bf16
    )
    probe_core = jnp.einsum("jbr,bp->jrp", k_left, sketch, preferred_element_type=f32).astype(bf16)
    a_up = a_low[..., :half_width]
    a_down = a_low[..., half_width:]

    def low_term(outer, inner, field):
        inner_core = jnp.einsum("ibr,bip->irp", inner, field, preferred_element_type=f32).astype(
            bf16
        )
        return jnp.einsum("ibr,irp->bip", outer, inner_core, preferred_element_type=f32)

    inner_first = jnp.einsum("ibr,bp->irp", a_down, sketch, preferred_element_type=f32).astype(bf16)
    a_first = jnp.einsum("ibr,irp->bip", a_up, inner_first, preferred_element_type=f32)
    piece = mixed_left
    terms = jnp.einsum("ijbs,jsp->bip", piece, probe_core, preferred_element_type=f32)
    first_share = summed_on_arrival(
        terms.reshape(share_count * lax.axis_size("cols"), rows_here * rank_cols), "cols", 0
    )
    own_first = (
        lax.dynamic_slice_in_dim(flatten_rows(a_first), share_offset, share_count, 0) - first_share
    )
    first_b = split_rows(collect(own_first.astype(bf16), "cols", 0))
    back_core = jnp.einsum(
        "ijbs,bip->ijsp", mixed_left, first_b, preferred_element_type=f32
    ).astype(bf16)
    a_second = low_term(a_down, a_up, first_b)
    piece = k_left
    terms = jnp.einsum("jbr,ijrp->bip", piece, back_core, preferred_element_type=f32)
    second_share = summed_on_arrival(
        terms.reshape(share_count * lax.axis_size("cols"), rows_here * rank_cols), "cols", 0
    )
    own_second = (
        lax.dynamic_slice_in_dim(flatten_rows(a_second), share_offset, share_count, 0)
        - second_share
    )
    second_b = split_rows(collect(own_second.astype(bf16), "cols", 0))
    fore_core = jnp.einsum("jbr,bip->ijrp", k_left, second_b, preferred_element_type=f32).astype(
        bf16
    )
    third_terms = jnp.einsum("ijbs,ijsp->bip", mixed_left, fore_core, preferred_element_type=f32)
    a_third = low_term(a_up, a_down, second_b)
    third = a_third - split_rows(total_of(flatten_rows(third_terms).astype(jnp.bfloat16), "cols"))
    gram_matrix = jnp.einsum("bip,biq->ipq", third, third, precision=lax.Precision.HIGHEST)
    basis_cols = apply_inverse(gram_matrix, third)
    basis_b = basis_cols.astype(bf16)
    last_core = jnp.einsum(
        "ijbs,bip->ijsp", mixed_left, basis_b, preferred_element_type=f32
    ).astype(bf16)
    last_terms = jnp.einsum("jbr,ijrp->bip", k_left, last_core, preferred_element_type=f32)
    projected = low_term(a_down, a_up, basis_b) - split_rows(
        total_of(flatten_rows(last_terms).astype(jnp.bfloat16), "cols")
    )
    solved = lax.linalg.triangular_solve(
        factor, flatten_rows(projected), left_side=True, lower=True
    )
    solved = split_rows(solved)
    panel_out = jnp.concatenate(
        [jnp.transpose(basis_cols, (1, 0, 2)), jnp.transpose(solved, (1, 0, 2))], axis=2
    )
    return (panel_out, diag_out)


def solution(mesh):
    return jax.shard_map(
        shards,
        mesh=mesh,
        in_specs=(
            P("rows", "cols", None, None),
            P("cols", "rows", None),
            P("rows", "cols"),
            P("rows", None, None),
            P("rows", None),
            P(),
        ),
        out_specs=(P("rows", None, None), P("rows", None)),
        check_vma=False,
    )
```

profile of v0, /device:TPU:1, one launch (start us, length us, event | category | flops | bytes accessed | tf_op | source)
XLA Modules:
  0.0 572.9 jit_solution(14631809102035162931)
XLA Ops:
  9.3 9.0 %all-to-all-start = ((bf16[8,3,128,128]{2,3,1,0:T(8,128)(2,1)}), bf16[8,3,128,128]{2,3,1,0:T(8,128)(2,1)S(1)}, u32[]{:S(2)}, u32[]{:S(2)}) async-start(bf16[8,3,128,128]{2,3,1,0:T(8,128)(2,1)} %broadcast_in_dim.16), calls=%async_computation | async-start | bytes 1572864 | tf_op jit(solution)/shard_map/all_to_all | solution.py:15
  19.0 22.9 %all-to-all-done = bf16[8,3,128,128]{2,3,1,0:T(8,128)(2,1)S(1)} async-done(((bf16[8,3,128,128]{2,3,1,0:T(8,128)(2,1)}), bf16[8,3,128,128]{2,3,1,0:T(8,128)(2,1)S(1)}, u32[]{:S(2)}, u32[]{:S(2)}) %all-to-all-start) | async-done | bytes 786464 | tf_op jit(solution)/shard_map/all_to_all | solution.py:15
  49.4 7.6 %all-to-all-start.1 = ((f32[32,32,128]{2,1,0:T(8,128)}), f32[32,32,128]{2,1,0:T(8,128)S(1)}, u32[]{:S(2)}, u32[]{:S(2)}) async-start(f32[32,32,128]{2,1,0:T(8,128)} %reshape_reshape.12), calls=%async_computation.1 | async-start | bytes 1048576 | tf_op jit(solution)/shard_map/all_to_all | solution.py:51
  60.2 8.4 %all-to-all-done.1 = f32[32,32,128]{2,1,0:T(8,128)S(1)} async-done(((f32[32,32,128]{2,1,0:T(8,128)}), f32[32,32,128]{2,1,0:T(8,128)S(1)}, u32[]{:S(2)}, u32[]{:S(2)}) %all-to-all-start.1) | async-done | bytes 524320 | tf_op jit(solution)/shard_map/all_to_all | solution.py:51
  73.6 7.9 %all-to-all-done.7 = bf16[32,4,1024]{2,1,0:T(4,128)(2,1)S(1)} async-done(((bf16[32,4,1024]{2,1,0:T(4,128)(2,1)}), bf16[32,4,1024]{2,1,0:T(4,128)(2,1)S(1)}, u32[]{:S(2)}, u32[]{:S(2)}) %all-to-all-start.7) | async-done | bytes 262176 | tf_op jit(solution)/shard_map/all_to_all | solution.py:31
  86.2 8.9 %all-to-all-done.2 = bf16[32,32,128]{2,1,0:T(8,128)(2,1)S(1)} async-done(((bf16[32,32,128]{2,1,0:T(8,128)(2,1)}), bf16[32,32,128]{2,1,0:T(8,128)(2,1)S(1)}, u32[]{:S(2)}, u32[]{:S(2)}) %all-to-all-start.2) | async-done | bytes 262176 | tf_op jit(solution)/shard_map/all_to_all | solution.py:15
  119.5 5.3 all-to-all-done.3
  132.5 7.1 %all-to-all-done.4 = bf16[32,32,128]{2,1,0:T(8,128)(2,1)S(1)} async-done(((bf16[32,32,128]{2,1,0:T(8,128)(2,1)}), bf16[32,32,128]{2,1,0:T(8,128)(2,1)S(1)}, u32[]{:S(2)}, u32[]{:S(2)}) %all-to-all-start.4) | async-done | bytes 262176 | tf_op jit(solution)/shard_map/all_to_all | solution.py:15
  141.2 12.5 %all_to_all.55 = bf16[32,32,128]{2,1,0:T(8,128)(2,1)S(1)} all-to-all(bf16[32,32,128]{2,1,0:T(8,128)(2,1)S(1)} %convert_element_type.133), channel_id=1, replica_groups=mesh['cols'=32,'rows'=8] {'cols'}, dimensions={0} | all-to-all | bytes 524288 | tf_op jit(solution)/shard_map/all_to_all | solution.py:31
  158.9 8.8 %all-to-all-done.6 = bf16[32,32,128]{2,1,0:T(8,128)(2,1)S(1)} async-done(((bf16[32,32,128]{2,1,0:T(8,128)(2,1)}), bf16[32,32,128]{2,1,0:T(8,128)(2,1)S(1)}, u32[]{:S(2)}, u32[]{:S(2)}) %all-to-all-start.6) | async-done | bytes 262176 | tf_op jit(solution)/shard_map/all_to_all | solution.py:15
  172.1 11.7 %custom-call.69 = f32[2,64,64]{2,1,0:T(8,128)S(1)} custom-call(f32[2,64,64]{2,1,0:T(8,128)S(1)} %fusion.144), custom_call_target="Cholesky" | custom-call | tf_op jit(solution)/shard_map/jit(cholesky)/cholesky | solution.py:56
  184.1 9.8 %custom-call.70 = f32[2,1,64,64]{2,3,1,0:T(8,128)S(1)} custom-call(f32[2,1,64,64]{3,2,1,0:T(8,128)S(1)} %select_bitcast_fusion.7), custom_call_target="InvertDiagBlocksLowerTriangular" | custom-call | tf_op jit(solution)/shard_map/triangular_solve | solution.py:57
  195.8 12.5 %all_to_all.56 = bf16[32,32,128]{2,1,0:T(8,128)(2,1)S(1)} all-to-all(bf16[32,32,128]{2,1,0:T(8,128)(2,1)S(1)} %convert_element_type.150), channel_id=1, replica_groups=mesh['cols'=32,'rows'=8] {'cols'}, dimensions={0} | all-to-all | bytes 524288 | tf_op jit(solution)/shard_map/all_to_all | solution.py:31
  212.9 9.0 %all-to-all-done.10 = bf16[32,32,128]{2,1,0:T(8,128)(2,1)S(1)} async-done(((bf16[32,32,128]{2,1,0:T(8,128)(2,1)}), bf16[32,32,128]{2,1,0:T(8,128)(2,1)S(1)}, u32[]{:S(2)}, u32[]{:S(2)}) %all-to-all-start.10) | async-done | bytes 262176 | tf_op jit(solution)/shard_map/all_to_all | solution.py:15
  233.4 11.7 %cholesky.250 = f32[128,128]{1,0:T(8,128)S(1)} custom-call(f32[128,128]{1,0:T(8,128)S(1)} %cholesky.616), custom_call_target="Cholesky" | custom-call | tf_op jit(solution)/shard_map/jit(cholesky)/cholesky | solution.py:94
  247.7 9.8 %custom-call.71 = f32[1,128,128]{1,2,0:T(8,128)S(1)} custom-call(f32[1,128,128]{2,1,0:T(8,128)S(1)} %get-tuple-element.84), custom_call_target="InvertDiagBlocksLowerTriangular" | custom-call | tf_op jit(solution)/shard_map/jit(cholesky)/cholesky | solution.py:94
  261.4 11.7 %cholesky.273 = f32[128,128]{1,0:T(8,128)S(1)} custom-call(f32[128,128]{1,0:T(8,128)S(1)} %cholesky.620), custom_call_target="Cholesky" | custom-call | tf_op jit(solution)/shard_map/jit(cholesky)/cholesky | solution.py:94
  273.8 10.0 %custom-call.72 = f32[1,128,128]{1,2,0:T(8,128)S(1)} custom-call(f32[1,128,128]{2,1,0:T(8,128)S(1)} %get-tuple-element.81), custom_call_target="InvertDiagBlocksLowerTriangular" | custom-call | tf_op jit(solution)/shard_map/jit(cholesky)/cholesky | solution.py:94
  287.1 11.7 %cholesky.504 = f32[128,128]{1,0:T(8,128)S(1)} custom-call(f32[128,128]{1,0:T(8,128)S(1)} %cholesky.625), custom_call_target="Cholesky" | custom-call | tf_op jit(solution)/shard_map/jit(cholesky)/cholesky | solution.py:94
  300.1 9.8 %custom-call.73 = f32[1,128,128]{1,2,0:T(8,128)S(1)} custom-call(f32[1,128,128]{2,1,0:T(8,128)S(1)} %get-tuple-element.78), custom_call_target="InvertDiagBlocksLowerTriangular" | custom-call | tf_op jit(solution)/shard_map/jit(cholesky)/cholesky | solution.py:94
  313.5 12.1 %cholesky.523 = f32[128,128]{1,0:T(8,128)S(1)} custom-call(f32[128,128]{1,0:T(8,128)S(1)} %cholesky.630), custom_call_target="Cholesky" | custom-call | tf_op jit(solution)/shard_map/jit(cholesky)/cholesky | solution.py:94
  326.9 9.8 %custom-call.74 = f32[1,128,128]{1,2,0:T(8,128)S(1)} custom-call(f32[1,128,128]{2,1,0:T(8,128)S(1)} %get-tuple-element.75), custom_call_target="InvertDiagBlocksLowerTriangular" | custom-call | tf_op jit(solution)/shard_map/jit(cholesky)/cholesky | solution.py:94
  340.1 11.7 %cholesky.542 = f32[128,128]{1,0:T(8,128)S(1)} custom-call(f32[128,128]{1,0:T(8,128)S(1)} %cholesky.635), custom_call_target="Cholesky" | custom-call | tf_op jit(solution)/shard_map/jit(cholesky)/cholesky | solution.py:94
  353.2 9.8 %custom-call.75 = f32[1,128,128]{1,2,0:T(8,128)S(1)} custom-call(f32[1,128,128]{2,1,0:T(8,128)S(1)} %get-tuple-element.72), custom_call_target="InvertDiagBlocksLowerTriangular" | custom-call | tf_op jit(solution)/shard_map/jit(cholesky)/cholesky | solution.py:94
  366.6 11.7 %cholesky.562 = f32[128,128]{1,0:T(8,128)S(1)} custom-call(f32[128,128]{1,0:T(8,128)S(1)} %cholesky.640), custom_call_target="Cholesky" | custom-call | tf_op jit(solution)/shard_map/jit(cholesky)/cholesky | solution.py:94
  379.5 9.8 %custom-call.76 = f32[1,128,128]{1,2,0:T(8,128)S(1)} custom-call(f32[1,128,128]{2,1,0:T(8,128)S(1)} %get-tuple-element.69), custom_call_target="InvertDiagBlocksLowerTriangular" | custom-call | tf_op jit(solution)/shard_map/jit(cholesky)/cholesky | solution.py:94
  392.4 11.7 %cholesky.582 = f32[128,128]{1,0:T(8,128)S(1)} custom-call(f32[128,128]{1,0:T(8,128)S(1)} %cholesky.645), custom_call_target="Cholesky" | custom-call | tf_op jit(solution)/shard_map/jit(cholesky)/cholesky | solution.py:94
  405.3 10.0 %custom-call.77 = f32[1,128,128]{1,2,0:T(8,128)S(1)} custom-call(f32[1,128,128]{2,1,0:T(8,128)S(1)} %get-tuple-element.66), custom_call_target="InvertDiagBlocksLowerTriangular" | custom-call | tf_op jit(solution)/shard_map/jit(cholesky)/cholesky | solution.py:94
  417.9 11.7 %cholesky.600 = f32[128,128]{1,0:T(8,128)S(1)} custom-call(f32[128,128]{1,0:T(8,128)S(1)} %convolution_subtract_fusion.11), custom_call_target="Cholesky" | custom-call | tf_op jit(solution)/shard_map/jit(cholesky)/cholesky | solution.py:94
  436.6 6.6 %fusion.1 = (f32[1024,1024]{1,0:T(8,128)}, f32[1024,1024]{1,0:T(8,128)}) fusion(f32[1024,1024]{1,0:T(8,128)} %get-tuple-element.64, pred[]{:T(512)S(6)} %cholesky.615), kind=kLoop, calls=%fused_computation.6 | loop fusion | flops 4194304 | bytes 12582913 | tf_op jit(solution)/shard_map/triangular_solve | solution.py:157
  443.2 27.5 %while.1 = (s32[]{:T(128)}, f32[1024,1024]{1,0:T(8,128)}, s32[8,2]{0,1:T(2,128)S(1)}, f32[8,128,128]{2,1,0:T(8,128)}, s32[]{:T(128)}) while((s32[]{:T(128)}, f32[1024,1024]{1,0:T(8,128)}, s32[8,2]{0,1:T(2,128)S(1)}, f32[8,128,128]{2,1,0:T(8,128)}, s32[]{:T(128)}) %tuple.73), condition=%wide.while_cond, body=%wide.while_body.sunk | while | flops 2 | bytes 132705 | solution.py:157
  470.7 79.6 %custom-call.78 = f32[8,128,128]{1,2,0:T(8,128)S(1)} custom-call(f32[8,128,128]{2,1,0:T(8,128)} %get-tuple-element.9), custom_call_target="InvertDiagBlocksLowerTriangular" | custom-call | tf_op jit(solution)/shard_map/triangular_solve | solution.py:157
  (173 shorter events, 161.9 us)
Async XLA Ops:
  7.2 37.9 %copy-start = (bf16[1024,64]{0,1:T(8,128)(2,1)S(1)}, bf16[1024,64]{0,1:T(8,128)(2,1)}, u32[]{:S(2)}) copy-start(bf16[1024,64]{0,1:T(8,128)(2,1)} %param.11) | copy-start | bytes 393220
  9.3 32.6 %all-to-all-start = ((bf16[8,3,128,128]{2,3,1,0:T(8,128)(2,1)}), bf16[8,3,128,128]{2,3,1,0:T(8,128)(2,1)S(1)}, u32[]{:S(2)}, u32[]{:S(2)}) async-start(bf16[8,3,128,128]{2,3,1,0:T(8,128)(2,1)} %broadcast_in_dim.16), calls=%async_computation | async-start | bytes 1572864 | tf_op jit(solution)/shard_map/all_to_all | solution.py:15
  42.0 15.0 %copy-start.1 = (bf16[2,1024,128]{2,1,0:T(8,128)(2,1)S(1)}, bf16[2,1024,128]{2,1,0:T(8,128)(2,1)}, u32[]{:S(2)}) copy-start(bf16[2,1024,128]{2,1,0:T(8,128)(2,1)} %param.9) | copy-start | bytes 1572868
  49.4 19.1 %all-to-all-start.1 = ((f32[32,32,128]{2,1,0:T(8,128)}), f32[32,32,128]{2,1,0:T(8,128)S(1)}, u32[]{:S(2)}, u32[]{:S(2)}) async-start(f32[32,32,128]{2,1,0:T(8,128)} %reshape_reshape.12), calls=%async_computation.1 | async-start | bytes 1048576 | tf_op jit(solution)/shard_map/all_to_all | solution.py:51
  68.6 13.0 %all-to-all-start.7 = ((bf16[32,4,1024]{2,1,0:T(4,128)(2,1)}), bf16[32,4,1024]{2,1,0:T(4,128)(2,1)S(1)}, u32[]{:S(2)}, u32[]{:S(2)}) async-start(bf16[32,4,1024]{2,1,0:T(4,128)(2,1)} %reshape.136), calls=%async_computation.7 | async-start | bytes 524288 | tf_op jit(solution)/shard_map/all_to_all | solution.py:31
  82.3 12.8 %all-to-all-start.2 = ((bf16[32,32,128]{2,1,0:T(8,128)(2,1)}), bf16[32,32,128]{2,1,0:T(8,128)(2,1)S(1)}, u32[]{:S(2)}, u32[]{:S(2)}) async-start(bf16[32,32,128]{2,1,0:T(8,128)(2,1)} %broadcast_in_dim.17), calls=%async_computation.2 | async-start | bytes 524288 | tf_op jit(solution)/shard_map/all_to_all | solution.py:15
  95.9 12.8 %all-to-all-start.8 = ((bf16[32,4,1024]{2,1,0:T(4,128)(2,1)}), bf16[32,4,1024]{2,1,0:T(4,128)(2,1)S(1)}, u32[]{:S(2)}, u32[]{:S(2)}) async-start(bf16[32,4,1024]{2,1,0:T(4,128)(2,1)} %broadcast_in_dim.20), calls=%async_computation.8 | async-start | bytes 524288 | tf_op jit(solution)/shard_map/all_to_all | solution.py:15
  108.6 16.1 %all-to-all-start.3 = ((f32[32,32,128]{2,1,0:T(8,128)}), f32[32,32,128]{2,1,0:T(8,128)}, u32[]{:S(2)}, u32[]{:S(2)}) async-start(f32[32,32,128]{2,1,0:T(8,128)} %reshape_reshape.14), calls=%async_computation.3 | async-start | bytes 1048576 | tf_op jit(solution)/shard_map/all_to_all | solution.py:51
  126.6 13.0 %all-to-all-start.4 = ((bf16[32,32,128]{2,1,0:T(8,128)(2,1)}), bf16[32,32,128]{2,1,0:T(8,128)(2,1)S(1)}, u32[]{:S(2)}, u32[]{:S(2)}) async-start(bf16[32,32,128]{2,1,0:T(8,128)(2,1)} %broadcast_in_dim.18), calls=%async_computation.4 | async-start | bytes 524288 | tf_op jit(solution)/shard_map/all_to_all | solution.py:15
  130.6 93.6 %all-gather.2.cloned.1.call-start = ((), (), s32[]{:S(2)}) async-start(), calls=%async_computation.11 | async-start | bytes 2359296 | tf_op jit(solution)/shard_map/all_gather | solution.py:91
  139.9 19.0 %copy-start.4 = (bf16[1024,2,64]{2,1,0:T(2,128)(2,1)}, bf16[1024,2,64]{2,1,0:T(2,128)(2,1)S(1)}, u32[]{:S(2)}) copy-start(bf16[1024,2,64]{2,1,0:T(2,128)(2,1)S(1)} %reshape_reshape.15) | copy-start | bytes 786436
  154.5 13.3 %all-to-all-start.6 = ((bf16[32,32,128]{2,1,0:T(8,128)(2,1)}), bf16[32,32,128]{2,1,0:T(8,128)(2,1)S(1)}, u32[]{:S(2)}, u32[]{:S(2)}) async-start(bf16[32,32,128]{2,1,0:T(8,128)(2,1)} %broadcast_in_dim.19), calls=%async_computation.6 | async-start | bytes 524288 | tf_op jit(solution)/shard_map/all_to_all | solution.py:15
  209.1 12.8 %all-to-all-start.10 = ((bf16[32,32,128]{2,1,0:T(8,128)(2,1)}), bf16[32,32,128]{2,1,0:T(8,128)(2,1)S(1)}, u32[]{:S(2)}, u32[]{:S(2)}) async-start(bf16[32,32,128]{2,1,0:T(8,128)(2,1)} %broadcast_in_dim.21), calls=%async_computation.10 | async-start | bytes 524288 | tf_op jit(solution)/shard_map/all_to_all | solution.py:15
  224.2 4.4 copy-start.3
  231.5 1.9 copy-start.2
Sparse Core Ops, SparseCore 0:
  133.2 39.5 all-gather.1
where the time goes:
time: 583 us; the launch traced here: 573 us
  other arithmetic  287 us (49%)
  waiting for transfers between devices  82.7 us (14%)
  local copies, waits for them, and re-layouts  64.7 us (11%)
  matrix products  48.5 us (8%)
  starting transfers between devices  44.7 us (8%)
  blocking collectives  24.9 us (4%)
  between operations  20.2 us (3%)
    another operation x30, other arithmetic, shards(): factor = jnp.linalg.cholesky(whole_diag)  172 us
    another operation x3, other arithmetic, shards(): lax.linalg.triangular_solve(factor, flatten_rows(projected), left_side=Tr...  86.2 us
    all_to_all x6, waiting for transfers between devices, from_everyone(): lax.all_to_all(jnp.broadcast_to(value[None], (count, *value.shape)), axis...  61 us
    all_to_all x6, starting transfers between devices, from_everyone(): lax.all_to_all(jnp.broadcast_to(value[None], (count, *value.shape)), axis...  28.7 us
    another operation x24, local copies, waits for them, and re-layouts  27.5 us
    all_to_all x2, blocking collectives, sum_at_owner(): blocks = lax.all_to_all(split_up(value, dim, count), axis, 0, 0, tiled=True)  24.9 us
    another operation x14, matrix products, shards(): factor = jnp.linalg.cholesky(whole_diag)  23.3 us
    all_to_all x2, waiting for transfers between devices, summed_on_arrival(): blocks = lax.all_to_all(split_up(value, dim, count), axis, 0, 0, tiled=True)  13.7 us
  transfers between devices with their start and end apart: 10, of which 9 were waited for; matrix products, arithmetic and copies ran while one was open for 9% of the time, Pallas kernels for 0%

commit v1 on v0

--- a/solution.py
+++ b/solution.py
@@ -1,8 +1,120 @@
+import functools
+
 import jax
 import jax.numpy as jnp
 from jax import lax
+from jax.experimental import pallas as pl
+from jax.experimental.pallas import tpu as pltpu
 from jax.sharding import PartitionSpec as P
 
+f32 = jnp.float32
+bf16 = jnp.bfloat16
+
+def rcp(p):
+    r = pl.reciprocal(p, approx=True)
+    return r * (2.0 - p * r)
+
+def strip_eliminate(parts, k0, s):
+    first = parts[0]
+    lanes = first.shape[1]
+    row = lax.broadcasted_iota(jnp.int32, (s, lanes), 0)
+    C = [jnp.broadcast_to(first[:, k0 + j:k0 + j + 1], (s, lanes)) for j in range(s)]
+    parts = list(parts)
+    diag = jnp.ones((s, lanes), f32)
+    for j in range(s):
+        p = C[j][j:j + 1, :]
+        diag = jnp.where(row == j, p, diag)
+        if j == s - 1: break
+        M = jnp.where(row > j, C[j] * rcp(p), 0.0)
+        for k in range(j + 1, s):
+            C[k] = C[k] - M * C[k][j:j + 1, :]
+        parts = [x - M * x[j:j + 1, :] for x in parts]
+    R = lax.rsqrt(diag)
+    return [x * R for x in parts]
+
+def tn(a, b, prec=None):
+    return lax.dot_general(a, b, (((0,), (0,)), ((), ())), preferred_element_type=f32, precision=prec)
+
+def chol_block(D, n, s, exact=False):
+    eye = (lax.broadcasted_iota(jnp.int32, (n, n), 0) == lax.broadcasted_iota(jnp.int32, (n, n), 1)).astype(f32)
+    WA, WE = D, eye
+    outU, outE = [], []
+    for k0 in range(0, n, s):
+        a, e = strip_eliminate([WA[:s], WE[:s]], k0, s)
+        outU.append(a); outE.append(e)
+        if k0 + s < n:
+            if exact:
+                lhs=a[:, k0 + s:]
+                WA = WA[s:] - tn(lhs, a, lax.Precision.HIGHEST)
+                WE = WE[s:] - tn(lhs, e, lax.Precision.HIGHEST)
+            else:
+                ab = a.astype(bf16); eb = e.astype(bf16)
+                lhs = ab[:, k0 + s:]
+                WA = WA[s:] - tn(lhs, ab)
+                WE = WE[s:] - tn(lhs, eb)
+    U = jnp.concatenate(outU, 0); E = jnp.concatenate(outE, 0)
+    i0=lax.broadcasted_iota(jnp.int32, (n, n), 0); i1=lax.broadcasted_iota(jnp.int32, (n, n), 1)
+    U = jnp.where(i1>=i0, U, 0.0)
+    return U, E
+
+
+def diag_kernel(a_ref, b_ref, slab_ref, x_ref, A, Y):
+    A[...] = a_ref[...].astype(f32)
+    Y[...] = b_ref[...]
+    N = a_ref.shape[0]
+    nb = N // 128
+    for kb in range(nb):
+        o = kb * 128
+        U, E = chol_block(A[o:o + 128, o:o + 128], 128, 16)
+        A[o:o + 128, o:o + 128] = U
+        Eb = E.astype(bf16)
+        y = jnp.dot(Eb, Y[o:o + 128, :].astype(bf16), preferred_element_type=f32)
+        x_ref[o:o + 128, :] = y
+        if o + 128 < N:
+            panel = jnp.dot(Eb, A[o:o + 128, o + 128:].astype(bf16), preferred_element_type=f32)
+            A[o:o + 128, o + 128:] = panel
+            pb = panel.astype(bf16)
+            for ib in range(kb + 1, nb):
+                r = ib * 128
+                A[r:r + 128, r:] -= tn(pb[:, r - o - 128:r - o], pb[:, r - o - 128:])
+            Y[o + 128:, :] -= tn(pb, y.astype(bf16))
+    z = lax.axis_index("rows")
+    row = z * 128 + lax.broadcasted_iota(jnp.int32, (128, 128), 0)
+    for kb in range(nb):
+        o = kb * 128
+        block = A[o:o + 128, pl.ds(pl.multiple_of(z * 128, 128), 128)].T
+        col = o + lax.broadcasted_iota(jnp.int32, (128, 128), 1)
+        slab_ref[:, o:o + 128] = jnp.where(col <= row, block, 0.0)
+
+
+def factor_and_solve(a, b):
+    vm = pl.BlockSpec(memory_space=pltpu.VMEM)
+    n = a.shape[0]
+    return pl.pallas_call(
+        diag_kernel,
+        out_shape=(jax.ShapeDtypeStruct((128, n), f32), jax.ShapeDtypeStruct(b.shape, f32)),
+        in_specs=[vm] * 2,
+        out_specs=[vm] * 2,
+        scratch_shapes=[pltpu.VMEM(a.shape, f32), pltpu.VMEM(b.shape, f32)],
+        compiler_params=pltpu.CompilerParams(vmem_limit_bytes=48 * 2**20),
+        name="diag",
+    )(a, b)
+
+
+def gram_kernel(g_ref, c_ref):
+    for i in range(g_ref.shape[0]):
+        c_ref[i] = chol_block(g_ref[i], 64, 16, exact=True)[1]
+
+
+def inverse_factors(grams):
+    vm = pl.BlockSpec(memory_space=pltpu.VMEM)
+    return pl.pallas_call(
+        gram_kernel,
+        out_shape=jax.ShapeDtypeStruct(grams.shape, f32),
+        in_specs=[vm],
+        out_specs=vm,
+        name="gram",
+    )(grams)
 
 def joined_along(blocks, dim):
     blocks = jnp.moveaxis(blocks, 0, dim)
@@ -53,11 +165,8 @@
 
 
 def apply_inverse(gram_matrix, field):
-    lower_factor = jnp.linalg.cholesky(gram_matrix)
-    turned = lax.linalg.triangular_solve(
-        lower_factor, jnp.transpose(field, (1, 2, 0)), left_side=True, lower=True
-    )
-    return jnp.transpose(turned, (2, 0, 1))
+    inverse = inverse_factors(gram_matrix)
+    return jnp.einsum("bip,iqp->biq", field, inverse, precision=lax.Precision.HIGHEST)
 
 
 def shards(panel, row_k, mask, a_low, a_diag, sketch):
@@ -90,10 +199,7 @@
     diag_sum = total_of(diag_part.astype(jnp.bfloat16), "cols")
     whole_diag = lax.all_gather(
         (a_diag - diag_sum).astype(jnp.bfloat16), "rows", axis=0, tiled=True
-    ).astype(jnp.float32)
-    factor = jnp.linalg.cholesky(whole_diag)
-    slab_rows = a_diag.shape[0]
-    diag_out = lax.dynamic_slice_in_dim(factor, lax.axis_index("rows") * slab_rows, slab_rows, 0)
+    )
     left_part = panel[..., :half_width]
     right_part = panel[..., half_width:]
     weights = mask.astype(f32)[:, :, None, None]
@@ -154,9 +260,7 @@
     projected = low_term(a_down, a_up, basis_b) - split_rows(
         total_of(flatten_rows(last_terms).astype(jnp.bfloat16), "cols")
     )
-    solved = lax.linalg.triangular_solve(
-        factor, flatten_rows(projected), left_side=True, lower=True
-    )
+    diag_out, solved = factor_and_solve(whole_diag, flatten_rows(projected))
     solved = split_rows(solved)
     panel_out = jnp.concatenate(
         [jnp.transpose(basis_cols, (1, 0, 2)), jnp.transpose(solved, (1, 0, 2))], axis=2

time: 583 us -> 253 us (0.43); the launches traced: 573 us -> 252 us
  other arithmetic: 287 us -> 2.25 us
  Pallas kernels: 0 us -> 42.9 us
  local copies, waits for them, and re-layouts: 64.7 us -> 22.6 us
  blocking collectives: 24.9 us -> 62.4 us
  matrix products: 48.5 us -> 14.2 us
  waiting for transfers between devices: 82.7 us -> 60.9 us
  starting transfers between devices: 44.7 us -> 32.4 us
    another operation x40 -> x0, other arithmetic: 280 us -> none  [the longest x30 172 us: shards(): factor = jnp.linalg.cholesky(whole_diag)]
    pallas_call x0 -> x2, Pallas kernels: none -> 42.9 us  [the longest x1 37.3 us: factor_and_solve(): pl.pallas_call(diag_kernel, out_shape=(jax.ShapeDtypeStruct((128, n), f32...]
    all_to_all x0 -> x3, blocking collectives: none -> 37.5 us  [from_everyone(): lax.all_to_all(jnp.broadcast_to(value[None], (count, *value.shape)), axis...]
    another operation x30 -> x0, matrix products: 35.5 us -> none  [the longest x14 23.3 us: shards(): factor = jnp.linalg.cholesky(whole_diag)]
    another operation x42 -> x0, local copies, waits for them, and re-layouts: 30.9 us -> none
    all_to_all x6 -> x3, waiting for transfers between devices: 61 us -> 38.6 us  [from_everyone(): lax.all_to_all(jnp.broadcast_to(value[None], (count, *value.shape)), axis...]
    all_to_all x6 -> x3, starting transfers between devices: 28.7 us -> 16.7 us  [from_everyone(): lax.all_to_all(jnp.broadcast_to(value[None], (count, *value.shape)), axis...]
  transfers between devices with their start and end apart: 10 -> 7, of which waited for: 9 -> 6; matrix products, arithmetic and copies ran while one was open for 9% -> 12% of each run, Pallas kernels for 0% -> 2%
where the time goes in v1:
time: 253 us; the launch traced here: 252 us
  blocking collectives  62.4 us (25%)
  waiting for transfers between devices  60.9 us (24%)
  Pallas kernels  42.9 us (17%)
  starting transfers between devices  32.4 us (13%)
  local copies, waits for them, and re-layouts  22.6 us (9%)
  between operations  14.4 us (6%)
  matrix products  14.2 us (6%)
    all_to_all x3, waiting for transfers between devices, from_everyone(): lax.all_to_all(jnp.broadcast_to(value[None], (count, *value.shape)), axis...  38.6 us
    all_to_all x3, blocking collectives, from_everyone(): lax.all_to_all(jnp.broadcast_to(value[None], (count, *value.shape)), axis...  37.5 us
    pallas_call x1, Pallas kernels, factor_and_solve(): pl.pallas_call(diag_kernel, out_shape=(jax.ShapeDtypeStruct((128, n), f32...  37.3 us
    all_to_all x2, blocking collectives, sum_at_owner(): blocks = lax.all_to_all(split_up(value, dim, count), axis, 0, 0, tiled=True)  24.9 us
    all_to_all x2, waiting for transfers between devices, summed_on_arrival(): blocks = lax.all_to_all(split_up(value, dim, count), axis, 0, 0, tiled=True)  19.1 us
    all_to_all x3, starting transfers between devices, from_everyone(): lax.all_to_all(jnp.broadcast_to(value[None], (count, *value.shape)), axis...  16.7 us
    all_to_all x2, starting transfers between devices, summed_on_arrival(): blocks = lax.all_to_all(split_up(value, dim, count), axis, 0, 0, tiled=True)  8 us
    all_to_all x1, starting transfers between devices, sum_at_owner(): blocks = lax.all_to_all(split_up(value, dim, count), axis, 0, 0, tiled=True)  7.58 us
  transfers between devices with their start and end apart: 7, of which 6 were waited for; matrix products, arithmetic and copies ran while one was open for 12% of the time, Pallas kernels for 2%

profile of v1, /device:TPU:1, one launch (start us, length us, event | category | flops | bytes accessed | tf_op | source)
XLA Modules:
  0.0 252.0 jit_solution(12455403016927502224)
XLA Ops:
  9.3 9.0 %all-to-all-start = ((bf16[8,3,128,128]{2,3,1,0:T(8,128)(2,1)}), bf16[8,3,128,128]{2,3,1,0:T(8,128)(2,1)S(1)}, u32[]{:S(2)}, u32[]{:S(2)}) async-start(bf16[8,3,128,128]{2,3,1,0:T(8,128)(2,1)} %broadcast_in_dim.12), calls=%async_computation | async-start | bytes 1572864 | tf_op jit(solution)/shard_map/all_to_all | solution.py:127
  18.3 23.6 %all-to-all-done = bf16[8,3,128,128]{2,3,1,0:T(8,128)(2,1)S(1)} async-done(((bf16[8,3,128,128]{2,3,1,0:T(8,128)(2,1)}), bf16[8,3,128,128]{2,3,1,0:T(8,128)(2,1)S(1)}, u32[]{:S(2)}, u32[]{:S(2)}) %all-to-all-start) | async-done | bytes 786464 | tf_op jit(solution)/shard_map/all_to_all | solution.py:127
  43.5 7.6 %all-to-all-start.7 = ((bf16[32,4,1024]{2,1,0:T(4,128)(2,1)}), bf16[32,4,1024]{2,1,0:T(4,128)(2,1)S(1)}, u32[]{:S(2)}, u32[]{:S(2)}) async-start(bf16[32,4,1024]{2,1,0:T(4,128)(2,1)} %reshape.53), calls=%async_computation.7 | async-start | bytes 524288 | tf_op jit(solution)/shard_map/all_to_all | solution.py:143
  51.1 3.1 %fusion.7 = bf16[2,3,1024,64]{2,3,1,0:T(8,128)(2,1)S(1)} fusion(bf16[2,3,1024,128]{3,2,1,0:T(8,128)(2,1)} %param.6, bf16[3,1024,128]{1,2,0:T(8,128)(2,1)S(1)} %copy_bitcast_fusion, f32[2,3]{1,0:T(2,128)S(1)} %convert_element_type.117), kind=kOutput, calls=%fused_computation.5 | convolution fusion | flops 101105664 | bytes 4326400 | tf_op jit(solution)/shard_map/ijbr,ijrs->ijbs/dot_general | solution.py:209
  55.5 1.4 reshape_reshape.12
  56.9 3.2 %all-to-all-done.7 = bf16[32,4,1024]{2,1,0:T(4,128)(2,1)S(1)} async-done(((bf16[32,4,1024]{2,1,0:T(4,128)(2,1)}), bf16[32,4,1024]{2,1,0:T(4,128)(2,1)S(1)}, u32[]{:S(2)}, u32[]{:S(2)}) %all-to-all-start.7) | async-done | bytes 262176 | tf_op jit(solution)/shard_map/all_to_all | solution.py:143
  60.0 4.2 %all-to-all-start.1 = ((f32[32,32,128]{2,1,0:T(8,128)}), f32[32,32,128]{2,1,0:T(8,128)S(1)}, u32[]{:S(2)}, u32[]{:S(2)}) async-start(f32[32,32,128]{2,1,0:T(8,128)} %reshape_reshape.12), calls=%async_computation.1 | async-start | bytes 1048576 | tf_op jit(solution)/shard_map/all_to_all | solution.py:163
  64.3 1.6 fusion.31
  66.0 9.8 %all-to-all-done.1 = f32[32,32,128]{2,1,0:T(8,128)S(1)} async-done(((f32[32,32,128]{2,1,0:T(8,128)}), f32[32,32,128]{2,1,0:T(8,128)S(1)}, u32[]{:S(2)}, u32[]{:S(2)}) %all-to-all-start.1) | async-done | bytes 524320 | tf_op jit(solution)/shard_map/all_to_all | solution.py:163
  76.6 4.0 %all-to-all-start.8 = ((bf16[32,4,1024]{2,1,0:T(4,128)(2,1)}), bf16[32,4,1024]{2,1,0:T(4,128)(2,1)S(1)}, u32[]{:S(2)}, u32[]{:S(2)}) async-start(bf16[32,4,1024]{2,1,0:T(4,128)(2,1)} %broadcast_in_dim.16), calls=%async_computation.8 | async-start | bytes 524288 | tf_op jit(solution)/shard_map/all_to_all | solution.py:127
  81.6 7.9 %all-to-all-done.8 = bf16[32,4,1024]{2,1,0:T(4,128)(2,1)S(1)} async-done(((bf16[32,4,1024]{2,1,0:T(4,128)(2,1)}), bf16[32,4,1024]{2,1,0:T(4,128)(2,1)S(1)}, u32[]{:S(2)}, u32[]{:S(2)}) %all-to-all-start.8) | async-done | bytes 262176 | tf_op jit(solution)/shard_map/all_to_all | solution.py:127
  90.3 3.8 %all-to-all-start.2 = ((bf16[32,32,128]{2,1,0:T(8,128)(2,1)}), bf16[32,32,128]{2,1,0:T(8,128)(2,1)S(1)}, u32[]{:S(2)}, u32[]{:S(2)}) async-start(bf16[32,32,128]{2,1,0:T(8,128)(2,1)} %broadcast_in_dim.13), calls=%async_computation.2 | async-start | bytes 524288 | tf_op jit(solution)/shard_map/all_to_all | solution.py:127
  94.2 1.8 subtract_convert_fusion
  96.0 7.1 %all-to-all-done.2 = bf16[32,32,128]{2,1,0:T(8,128)(2,1)S(1)} async-done(((bf16[32,32,128]{2,1,0:T(8,128)(2,1)}), bf16[32,32,128]{2,1,0:T(8,128)(2,1)S(1)}, u32[]{:S(2)}, u32[]{:S(2)}) %all-to-all-start.2) | async-done | bytes 262176 | tf_op jit(solution)/shard_map/all_to_all | solution.py:127
  103.9 1.3 copy.46
  105.2 2.6 %reshape_reshape.14 = f32[32,32,128]{2,1,0:T(8,128)} reshape(f32[1024,2,64]{2,1,0:T(2,128)} %copy.46) | data formatting | bytes 1048576 | tf_op jit(solution)/shard_map/reshape;reshape | solution.py:138
  107.8 3.8 %all-to-all-start.3 = ((f32[32,32,128]{2,1,0:T(8,128)}), f32[32,32,128]{2,1,0:T(8,128)S(1)}, u32[]{:S(2)}, u32[]{:S(2)}) async-start(f32[32,32,128]{2,1,0:T(8,128)} %reshape_reshape.14), calls=%async_computation.3 | async-start | bytes 1048576 | tf_op jit(solution)/shard_map/all_to_all | solution.py:163
  111.6 1.4 fusion.32
  114.0 9.3 %all-to-all-done.3 = f32[32,32,128]{2,1,0:T(8,128)S(1)} async-done(((f32[32,32,128]{2,1,0:T(8,128)}), f32[32,32,128]{2,1,0:T(8,128)S(1)}, u32[]{:S(2)}, u32[]{:S(2)}) %all-to-all-start.3) | async-done | bytes 524320 | tf_op jit(solution)/shard_map/all_to_all | solution.py:163
  123.4 12.6 %all_to_all.55 = bf16[32,32,128]{2,1,0:T(8,128)(2,1)S(1)} all-to-all(bf16[32,32,128]{2,1,0:T(8,128)(2,1)S(1)} %broadcast_in_dim.14), channel_id=1, replica_groups=mesh['cols'=32,'rows'=8] {'cols'}, dimensions={0} | all-to-all | bytes 524288 | tf_op jit(solution)/shard_map/all_to_all | solution.py:127
  137.6 12.5 %all_to_all.56 = bf16[32,32,128]{2,1,0:T(8,128)(2,1)S(1)} all-to-all(bf16[32,32,128]{2,1,0:T(8,128)(2,1)S(1)} %convert_element_type.130), channel_id=1, replica_groups=mesh['cols'=32,'rows'=8] {'cols'}, dimensions={0} | all-to-all | bytes 524288 | tf_op jit(solution)/shard_map/all_to_all | solution.py:143
  150.1 12.5 %all_to_all.57 = bf16[32,32,128]{2,1,0:T(8,128)(2,1)S(1)} all-to-all(bf16[32,32,128]{2,1,0:T(8,128)(2,1)S(1)} %broadcast_in_dim.15), channel_id=1, replica_groups=mesh['cols'=32,'rows'=8] {'cols'}, dimensions={0} | all-to-all | bytes 524288 | tf_op jit(solution)/shard_map/all_to_all | solution.py:127
  164.4 1.8 fusion.10
  167.4 5.6 %gram.1 = f32[2,64,64]{2,1,0:T(8,128)} custom-call(f32[2,64,64]{2,1,0:T(8,128)} %fusion.84.g_ref), custom_call_target="tpu_custom_call" | custom-call | tf_op jit(solution)/shard_map/gram/pallas_call | solution.py:111
  173.0 1.4 fusion.85
  175.7 12.5 %all_to_all.58 = bf16[32,32,128]{2,1,0:T(8,128)(2,1)S(1)} all-to-all(bf16[32,32,128]{2,1,0:T(8,128)(2,1)S(1)} %convert_element_type.146), channel_id=1, replica_groups=mesh['cols'=32,'rows'=8] {'cols'}, dimensions={0} | all-to-all | bytes 524288 | tf_op jit(solution)/shard_map/all_to_all | solution.py:143
  188.2 12.5 %all_to_all.59 = bf16[32,32,128]{2,1,0:T(8,128)(2,1)S(1)} all-to-all(bf16[32,32,128]{2,1,0:T(8,128)(2,1)S(1)} %broadcast_in_dim.17), channel_id=1, replica_groups=mesh['cols'=32,'rows'=8] {'cols'}, dimensions={0} | all-to-all | bytes 524288 | tf_op jit(solution)/shard_map/all_to_all | solution.py:127
  200.7 1.6 reshape.58
  202.3 1.7 copy.55
  204.6 1.6 copy-done.1
  206.2 37.3 %diag.1 = (f32[128,1024]{1,0:T(8,128)}, f32[1024,128]{1,0:T(8,128)S(1)}) custom-call(bf16[1024,1024]{1,0:T(8,128)(2,1)S(1)} %copy-done.1, f32[1024,128]{1,0:T(8,128)S(1)} %copy.56.b_ref), custom_call_target="tpu_custom_call" | custom-call | tf_op jit(solution)/shard_map/diag/pallas_call | solution.py:93
  243.8 1.3 copy.58
  (54 shorter events, 16.6 us)
Async XLA Ops:
  7.2 47.0 %copy-start = (bf16[1024,64]{0,1:T(8,128)(2,1)S(1)}, bf16[1024,64]{0,1:T(8,128)(2,1)}, u32[]{:S(2)}) copy-start(bf16[1024,64]{0,1:T(8,128)(2,1)} %param.11) | copy-start | bytes 393220
  7.2 11.1 %copy-start.4 = (s32[2,3]{1,0:T(2,128)S(1)}, s32[2,3]{1,0:T(2,128)}, u32[]{:S(2)}) copy-start(s32[2,3]{1,0:T(2,128)} %param.8) | copy-start | bytes 76
  9.3 32.6 %all-to-all-start = ((bf16[8,3,128,128]{2,3,1,0:T(8,128)(2,1)}), bf16[8,3,128,128]{2,3,1,0:T(8,128)(2,1)S(1)}, u32[]{:S(2)}, u32[]{:S(2)}) async-start(bf16[8,3,128,128]{2,3,1,0:T(8,128)(2,1)} %broadcast_in_dim.12), calls=%async_computation | async-start | bytes 1572864 | tf_op jit(solution)/shard_map/all_to_all | solution.py:127
  43.5 16.5 %all-to-all-start.7 = ((bf16[32,4,1024]{2,1,0:T(4,128)(2,1)}), bf16[32,4,1024]{2,1,0:T(4,128)(2,1)S(1)}, u32[]{:S(2)}, u32[]{:S(2)}) async-start(bf16[32,4,1024]{2,1,0:T(4,128)(2,1)} %reshape.53), calls=%async_computation.7 | async-start | bytes 524288 | tf_op jit(solution)/shard_map/all_to_all | solution.py:143
  55.4 8.8 %copy-start.2 = (bf16[2,1024,128]{2,1,0:T(8,128)(2,1)S(1)}, bf16[2,1024,128]{2,1,0:T(8,128)(2,1)}, u32[]{:S(2)}) copy-start(bf16[2,1024,128]{2,1,0:T(8,128)(2,1)} %param.9) | copy-start | bytes 1572868
  60.0 15.8 %all-to-all-start.1 = ((f32[32,32,128]{2,1,0:T(8,128)}), f32[32,32,128]{2,1,0:T(8,128)S(1)}, u32[]{:S(2)}, u32[]{:S(2)}) async-start(f32[32,32,128]{2,1,0:T(8,128)} %reshape_reshape.12), calls=%async_computation.1 | async-start | bytes 1048576 | tf_op jit(solution)/shard_map/all_to_all | solution.py:163
  76.6 13.0 %all-to-all-start.8 = ((bf16[32,4,1024]{2,1,0:T(4,128)(2,1)}), bf16[32,4,1024]{2,1,0:T(4,128)(2,1)S(1)}, u32[]{:S(2)}, u32[]{:S(2)}) async-start(bf16[32,4,1024]{2,1,0:T(4,128)(2,1)} %broadcast_in_dim.16), calls=%async_computation.8 | async-start | bytes 524288 | tf_op jit(solution)/shard_map/all_to_all | solution.py:127
  90.3 12.8 %all-to-all-start.2 = ((bf16[32,32,128]{2,1,0:T(8,128)(2,1)}), bf16[32,32,128]{2,1,0:T(8,128)(2,1)S(1)}, u32[]{:S(2)}, u32[]{:S(2)}) async-start(bf16[32,32,128]{2,1,0:T(8,128)(2,1)} %broadcast_in_dim.13), calls=%async_computation.2 | async-start | bytes 524288 | tf_op jit(solution)/shard_map/all_to_all | solution.py:127
  94.1 110.5 %all-gather.2.cloned.1.call-start = ((), (), s32[]{:S(2)}) async-start(), calls=%async_computation.11 | async-start | bytes 2359296 | tf_op jit(solution)/shard_map/all_gather | solution.py:200
  107.8 15.4 %all-to-all-start.3 = ((f32[32,32,128]{2,1,0:T(8,128)}), f32[32,32,128]{2,1,0:T(8,128)S(1)}, u32[]{:S(2)}, u32[]{:S(2)}) async-start(f32[32,32,128]{2,1,0:T(8,128)} %reshape_reshape.14), calls=%async_computation.3 | async-start | bytes 1048576 | tf_op jit(solution)/shard_map/all_to_all | solution.py:163
  136.2 1.4 copy-start.3
  204.6 1.6 copy-start.1
Sparse Core Ops, SparseCore 0:
  96.7 33.5 all-gather.1

commit v2 on v1

v2 whole, which is shorter than its diff:
```python
import functools

import jax
import jax.numpy as jnp
from jax import lax
from jax.experimental import pallas as pl
from jax.experimental.pallas import tpu as pltpu
from jax.sharding import PartitionSpec as P

f32 = jnp.float32
bf16 = jnp.bfloat16
MESH = pl.DeviceIdType.MESH
HIGHEST = lax.Precision.HIGHEST

def rcp(p):
    r = pl.reciprocal(p, approx=True)
    return r * (2.0 - p * r)

def strip_eliminate(parts, k0, s):
    first = parts[0]
    lanes = first.shape[1]
    row = lax.broadcasted_iota(jnp.int32, (s, lanes), 0)
    C = [jnp.broadcast_to(first[:, k0 + j:k0 + j + 1], (s, lanes)) for j in range(s)]
    parts = list(parts)
    diag = jnp.ones((s, lanes), f32)
    for j in range(s):
        p = C[j][j:j + 1, :]
        diag = jnp.where(row == j, p, diag)
        if j == s - 1: break
        M = jnp.where(row > j, C[j] * rcp(p), 0.0)
        for k in range(j + 1, s):
            C[k] = C[k] - M * C[k][j:j + 1, :]
        parts = [x - M * x[j:j + 1, :] for x in parts]
    R = lax.rsqrt(diag)
    return [x * R for x in parts]

def tn(a, b, prec=None):
    return lax.dot_general(a, b, (((0,), (0,)), ((), ())), preferred_element_type=f32, precision=prec)

def chol_block(D, n, s, exact=False):
    eye = (lax.broadcasted_iota(jnp.int32, (n, n), 0) == lax.broadcasted_iota(jnp.int32, (n, n), 1)).astype(f32)
    WA, WE = D, eye
    outU, outE = [], []
    for k0 in range(0, n, s):
        a, e = strip_eliminate([WA[:s], WE[:s]], k0, s)
        outU.append(a); outE.append(e)
        if k0 + s < n:
            if exact:
                lhs=a[:, k0 + s:]
                WA = WA[s:] - tn(lhs, a, lax.Precision.HIGHEST)
                WE = WE[s:] - tn(lhs, e, lax.Precision.HIGHEST)
            else:
                ab = a.astype(bf16); eb = e.astype(bf16)
                lhs = ab[:, k0 + s:]
                WA = WA[s:] - tn(lhs, ab)
                WE = WE[s:] - tn(lhs, eb)
    U = jnp.concatenate(outU, 0); E = jnp.concatenate(outE, 0)
    i0=lax.broadcasted_iota(jnp.int32, (n, n), 0); i1=lax.broadcasted_iota(jnp.int32, (n, n), 1)
    U = jnp.where(i1>=i0, U, 0.0)
    return U, E


def inverse_pair(gram):
    n, s = 64, 16
    low = lax.broadcasted_iota(jnp.int32, (s, 128), 1) < n
    row = lax.broadcasted_iota(jnp.int32, (s, 128), 0)
    lanes = lax.broadcasted_iota(jnp.int32, (n, 128), 1)
    left = lanes < n
    A = jnp.where(left, gram[:n], gram[n:])
    E = (lax.rem(lanes, n) == lax.broadcasted_iota(jnp.int32, (n, 128), 0)).astype(f32)
    done = []
    for k0 in range(0, n, s):
        a, e = A[:s], E[:s]
        C = [
            jnp.where(
                low,
                jnp.broadcast_to(a[:, k0 + j:k0 + j + 1], (s, 128)),
                jnp.broadcast_to(a[:, n + k0 + j:n + k0 + j + 1], (s, 128)),
            )
            for j in range(s)
        ]
        diag = jnp.ones((s, 128), f32)
        for j in range(s):
            p = C[j][j:j + 1, :]
            diag = jnp.where(row == j, p, diag)
            if j == s - 1:
                break
            r = rcp(p)
            r = r * (2.0 - p * r)
            M = jnp.where(row > j, C[j] * r, 0.0)
            for k in range(j + 1, s):
                C[k] = C[k] - M * C[k][j:j + 1, :]
            a = a - M * a[j:j + 1, :]
            e = e - M * e[j:j + 1, :]
        R = lax.rsqrt(diag)
        a, e = a * R, e * R
        done.append(e)
        if k0 + s < n:
            both = tn(a, jnp.concatenate([a, e], axis=1), HIGHEST)
            both = [both[:, :128], both[:, 128:]]
            keep = left[k0 + s:]
            step = [jnp.where(keep, x[k0 + s:n], x[n + k0 + s:]) for x in both]
            A, E = A[s:] - step[0], E[s:] - step[1]
    E = jnp.concatenate(done, axis=0)
    return jnp.concatenate([jnp.where(left, E, 0.0), jnp.where(left, 0.0, E)], axis=0)


def nn(a, b, prec=None):
    return jnp.dot(a, b, preferred_element_type=f32, precision=prec)


def nt(a, b, prec=None):
    return lax.dot_general(a, b, (((1,), (1,)), ((), ())), preferred_element_type=f32, precision=prec)


def low_lanes(n):
    return lax.broadcasted_iota(jnp.int32, (n, 128), 1) < 64


def sketch_kernel(
    panel, row_k, mask, a_low, a_diag, sketch,
    basis_ref, proj_ref, full,
    ROW, LT, ACC, MIX, S2, DP, DRS, FULL, TS, RS, FB, SB, TH, PB,
    zsend, zrecv, dsend, drecv, csend, crecv, rsend, rrecv, asend, arecv,
    *, NC, NR,
):
    B = NR * 128
    share = B // NC
    strips = 8
    wide = B // (NC // strips)
    c = lax.axis_index("cols")
    z = lax.axis_index("rows")
    base = pl.multiple_of(c * share, share)
    barrier = pltpu.get_barrier_semaphore()

    def col_of(d):
        return lax.rem(c + d, NC)

    def row_of(d):
        return lax.rem(z + d + NR, NR)

    def each(n, body):
        def step(d, carry):
            body(d)
            return carry
        lax.fori_loop(1, n, step, 0)

    each(NC, lambda d: pl.semaphore_signal(barrier, 1, device_id={"cols": col_of(d)}, device_id_type=MESH))
    each(NR, lambda d: pl.semaphore_signal(barrier, 1, device_id={"rows": row_of(d)}, device_id_type=MESH))

    S2[...] = jnp.concatenate([sketch[...], sketch[...]], axis=1)
    for i in range(2):
        LT[384 + 128 * i:512 + 128 * i, :] = a_low[i].T
    for j in range(3):
        ROW[j, pl.ds(pl.multiple_of(z * 128, 128), 128), :] = row_k[j]
        ACC[j] = jnp.zeros_like(ACC[j])
    pl.semaphore_wait(barrier, NC + NR - 2)

    def slab(owner):
        return pl.ds(pl.multiple_of(owner * 128, 128), 128)

    def hop(way, step, owner):
        place = ROW.at[:, slab(owner), :]
        return pltpu.make_async_remote_copy(
            src_ref=place, dst_ref=place,
            send_sem=zsend.at[way, step], recv_sem=zrecv.at[way, step],
            device_id={"rows": row_of(1 if way == 0 else -1)}, device_id_type=MESH,
        )

    def absorb(owner):
        for j in range(3):
            r = ROW[j, slab(owner), :]
            rt = r.T
            LT[640 + 128 * j:768 + 128 * j, slab(owner)] = rt
            right = jnp.concatenate(
                [panel[0, j, slab(owner), :], panel[1, j, slab(owner), :], r, S2[slab(owner), :]], axis=1
            )
            ACC[j] += nn(rt, right)

    ups, downs = NR // 2, NR - 1 - NR // 2
    hops = [hop(0, 0, z)] + ([hop(1, 0, z)] if downs else [])
    for h in hops:
        h.start()
    absorb(z)
    for s in range(ups):
        arrived = [row_of(-1 - s)]
        hop(0, s, arrived[0]).wait_recv()
        if s + 1 < ups:
            h = hop(0, s + 1, arrived[0])
            h.start()
            hops.append(h)
        if s < downs:
            arrived.append(row_of(1 + s))
            hop(1, s, arrived[1]).wait_recv()
            if s + 1 < downs:
                h = hop(1, s + 1, arrived[1])
                h.start()
                hops.append(h)
        for owner in arrived:
            absorb(owner)

    part = jnp.zeros((128, B), f32)
    for j in range(3):
        core = pltpu.roll(ACC[j, 64:128, 256:384], 64, 1)
        core = jnp.where(low_lanes(64), core, 0.0).astype(bf16)
        core = jnp.concatenate([core, jnp.zeros((64, 128), bf16)], axis=0)
        own = nn(ROW[j, slab(z), :], core).astype(bf16)
        part = part + nn(own, LT[640 + 128 * j:768 + 128 * j, :])
    DP[...] = part.astype(bf16)

    def piece(owner):
        return (
            pl.ds(pl.multiple_of(lax.rem(owner, strips) * 16, 16), 16),
            pl.ds(pl.multiple_of(lax.div(owner, strips) * wide, 128), wide),
        )

    def send_diag(d):
        rows, columns = piece(col_of(d))
        pltpu.make_async_remote_copy(
            src_ref=DP.at[rows, columns], dst_ref=DRS.at[d - 1],
            send_sem=dsend.at[0], recv_sem=drecv.at[0],
            device_id={"cols": col_of(d)}, device_id_type=MESH,
        ).start()

    def all_in(ref, sem):
        pltpu.make_async_copy(ref, ref, sem).wait()

    each(NC, send_diag)

    weight = []
    for i in range(2):
        for j in range(3):
            block = ACC[j, :, 128 * i:128 * i + 128] * mask[i, j].astype(f32)
            flat = jnp.where(low_lanes(64), pltpu.roll(block[64:, :], 64, 1), 0.0).astype(bf16)
            m = 3 * i + j
            turned = block.T[64:, :]
            if m % 2 == 0:
                turned = jnp.where(low_lanes(64), pltpu.roll(turned, 64, 1), 0.0)
            else:
                turned = jnp.where(low_lanes(64), 0.0, turned)
            weight.append(jnp.concatenate([turned.astype(bf16), jnp.zeros((64, 128), bf16)], axis=0))
            LT[64 * m:64 * m + 64, :] = nt(flat, panel[i, j]).astype(bf16)
    for t in range(3):
        m, n = 2 * t, 2 * t + 1
        MIX[:, 128 * t:128 * t + 128] = (
            nn(panel[m // 3, m % 3], weight[m]) + nn(panel[n // 3, n % 3], weight[n])
        ).astype(bf16)

    def spread(inner):
        keep = low_lanes(192)
        zero = jnp.zeros_like(inner)
        return jnp.concatenate([jnp.where(keep, inner, zero), jnp.where(keep, zero, inner)], axis=0)

    def start_sum(n, terms):
        TS[n] = terms
        def send(d):
            pltpu.make_async_remote_copy(
                src_ref=TS.at[n, pl.ds(pl.multiple_of(col_of(d) * share, share), share), :],
                dst_ref=RS.at[n, d - 1],
                send_sem=rsend.at[n], recv_sem=rrecv.at[n],
                device_id={"cols": col_of(d)}, device_id_type=MESH,
            ).start()
        each(NC, send)

    def end_sum(n):
        all_in(RS.at[n], rrecv.at[n])
        return TS[n, pl.ds(base, share), :] + jnp.sum(RS[n], axis=0)

    def start_gather(n, whole, own):
        place = whole.at[pl.ds(base, share), :]
        place[...] = own
        def send(d):
            pltpu.make_async_remote_copy(
                src_ref=place, dst_ref=place, send_sem=asend.at[n], recv_sem=arecv.at[n],
                device_id={"cols": col_of(d)}, device_id_type=MESH,
            ).start()
        each(NC, send)

    def end_gather(n, whole):
        all_in(whole.at[pl.ds(0, B - share), :], arecv.at[n])

    def low_share(inner, up):
        total = jnp.zeros((share, 128), f32)
        zero = jnp.zeros((64, 128), bf16)
        for i in range(2):
            half = inner[128 * i + 64:128 * i + 128] if up else inner[128 * i:128 * i + 64]
            keep = low_lanes(64) if i == 0 else jnp.logical_not(low_lanes(64))
            half = jnp.where(keep, half, 0.0).astype(bf16)
            right = jnp.concatenate([half, zero] if up else [zero, half], axis=0)
            total = total + nn(a_low[i, pl.ds(base, share), :], right)
        return total

    def back_terms(back):
        zero = jnp.zeros((64, 128), bf16)
        total = jnp.zeros((B, 128), f32)
        for j in range(3):
            mine = jnp.where(low_lanes(64), back[64 * j:64 * j + 64], back[192 + 64 * j:256 + 64 * j])
            total = total + nn(ROW[j], jnp.concatenate([mine.astype(bf16), zero], axis=0))
        return total

    probe = jnp.concatenate([ACC[j, :64, 384:512] for j in range(3)], axis=0)
    start_sum(0, nn(MIX[...], spread(probe).astype(bf16)))
    low = low_share(nn(LT[384:640, :], S2[...]), True)
    all_in(DRS, drecv.at[0])
    rows, columns = piece(c)
    own = a_diag[rows, columns] - (
        DP[rows, columns].astype(f32) + jnp.sum(DRS[...].astype(f32), axis=0)
    )
    strip = lax.rem(c, strips)
    pair, core = lax.div(strip, 2), lax.rem(strip, 2)
    FULL[z, pair, core, :, columns] = own.astype(bf16)

    def send_rows(d):
        place = FULL.at[z, pair, core, :, columns]
        pltpu.make_async_remote_copy(
            src_ref=place, dst_ref=place, send_sem=dsend.at[1], recv_sem=drecv.at[1],
            device_id={"rows": row_of(d)}, device_id_type=MESH,
        ).start()

    each(NR, send_rows)
    start_gather(0, FB, (low - end_sum(0)).astype(bf16))
    all_in(FULL.at[pl.ds(0, NR - 1), pair, core, :, columns], drecv.at[1])
    end_gather(0, FB)

    inner = nn(LT[:640, :], FB[...])
    start_sum(1, back_terms(inner[:384]))

    def to_chip(d):
        place = FULL.at[:, pair, core, :, columns]
        return pltpu.make_async_remote_copy(
            src_ref=place, dst_ref=place, send_sem=csend.at[d - 1], recv_sem=crecv.at[d - 1],
            device_id={"cols": lax.rem(c + 2 * d, NC)}, device_id_type=MESH,
        )

    each(NC // 2, lambda d: to_chip(d).start())
    low = low_share(inner[384:], False)
    start_gather(1, SB, (low - end_sum(1)).astype(bf16))
    end_gather(1, SB)

    inner = nn(LT[384:, :], SB[...])
    fore = jnp.concatenate([inner[256 + 128 * j:320 + 128 * j] for j in range(3)], axis=0)
    start_sum(2, nn(MIX[...], spread(fore).astype(bf16)))
    low = low_share(inner[:256], True)
    each(NC // 2, lambda d: to_chip(d).wait_recv())
    place = FULL.at[:, :, core]
    to_core = pltpu.make_async_remote_copy(
        src_ref=place, dst_ref=place, send_sem=dsend.at[2], recv_sem=drecv.at[2],
        device_id={"cols": c + 1 - 2 * core}, device_id_type=MESH,
    )
    to_core.start()
    start_gather(2, TH, low - end_sum(2))
    end_gather(2, TH)

    third = TH[...]
    basis = nt(third, inverse_pair(nn(third.T, third, HIGHEST)), HIGHEST)
    basis_ref[...] = basis

    inner = nn(LT[:640, :], basis.astype(bf16))
    start_sum(3, back_terms(inner[:384]))
    low = low_share(inner[384:], False)
    start_gather(3, PB, (low - end_sum(3)).astype(bf16))
    to_core.wait_recv()
    full[...] = FULL[...]
    end_gather(3, PB)
    proj_ref[...] = PB[...]

    for h in hops:
        h.wait_send()
    all_in(DRS, dsend.at[0])
    all_in(FULL.at[pl.ds(0, NR - 1), pair, core, :, columns], dsend.at[1])
    each(NC // 2, lambda d: to_chip(d).wait_send())
    to_core.wait_send()
    for n in range(4):
        all_in(RS.at[n], rsend.at[n])
    for n, whole in enumerate((FB, SB, TH, PB)):
        all_in(whole.at[pl.ds(0, B - share), :], asend.at[n])


def sketch_sums(panel, row_k, mask, a_low, a_diag, sketch):
    NC, NR = lax.axis_size("cols"), lax.axis_size("rows")
    B = NR * 128
    share = B // NC
    wide = B // (NC // 8)
    vm = pl.BlockSpec(memory_space=pltpu.VMEM)
    dma = pltpu.SemaphoreType.DMA
    shape = jax.ShapeDtypeStruct
    return pl.pallas_call(
        functools.partial(sketch_kernel, NC=NC, NR=NR),
        out_shape=(
            shape((B, 128), f32), shape((B, 128), bf16), shape((NR, 4, 2, 16, B), bf16),
        ),
        in_specs=[vm, vm, pl.BlockSpec(memory_space=pltpu.SMEM), vm, vm, vm],
        out_specs=[vm] * 3,
        scratch_shapes=[
            pltpu.VMEM((3, B, 128), bf16),
            pltpu.VMEM((1024, B), bf16),
            pltpu.VMEM((3, 128, 512), f32),
            pltpu.VMEM((B, 384), bf16),
            pltpu.VMEM((B, 128), bf16),
            pltpu.VMEM((128, B), bf16),
            pltpu.VMEM((NC - 1, 16, wide), bf16),
            pltpu.VMEM((NR, 4, 2, 16, B), bf16),
            pltpu.VMEM((4, B, 128), f32),
            pltpu.VMEM((4, NC - 1, share, 128), f32),
            pltpu.VMEM((B, 128), bf16),
            pltpu.VMEM((B, 128), bf16),
            pltpu.VMEM((B, 128), f32),
            pltpu.VMEM((B, 128), bf16),
            dma((2, 4)), dma((2, 4)), dma((3,)), dma((3,)),
            dma((NC // 2,)), dma((NC // 2,)),
            dma((4,)), dma((4,)), dma((4,)), dma((4,)),
        ],
        compiler_params=pltpu.CompilerParams(
            collective_id=0, has_side_effects=True, vmem_limit_bytes=50 * 2**20
        ),
        name="sketches",
    )(panel, row_k, mask, a_low, a_diag, sketch)


def diag_kernel(a_ref, proj_ref, basis_ref, panel_ref, slab_ref, A, Y):
    A[...] = a_ref[...].astype(f32)
    Y[...] = proj_ref[...].astype(f32)
    N = a_ref.shape[0]
    nb = N // 128
    left = lax.broadcasted_iota(jnp.int32, (128, 128), 1) < 64
    for kb in range(nb):
        o = kb * 128
        U, E = chol_block(A[o:o + 128, o:o + 128], 128, 16)
        A[o:o + 128, o:o + 128] = U
        Eb = E.astype(bf16)
        y = nn(Eb, Y[o:o + 128, :].astype(bf16))
        basis = basis_ref[o:o + 128, :]
        panel_ref[0, o:o + 128, :] = jnp.where(left, basis, pltpu.roll(y, 64, 1))
        panel_ref[1, o:o + 128, :] = jnp.where(left, pltpu.roll(basis, 64, 1), y)
        if o + 128 < N:
            panel = nn(Eb, A[o:o + 128, o + 128:].astype(bf16))
            A[o:o + 128, o + 128:] = panel
            pb = panel.astype(bf16)
            for ib in range(kb + 1, nb):
                r = ib * 128
                A[r:r + 128, r:] -= tn(pb[:, r - o - 128:r - o], pb[:, r - o - 128:])
            Y[o + 128:, :] -= tn(pb, y.astype(bf16))
    z = lax.axis_index("rows")
    row = z * 128 + lax.broadcasted_iota(jnp.int32, (128, 128), 0)
    for kb in range(nb):
        o = kb * 128
        block = A[o:o + 128, pl.ds(pl.multiple_of(z * 128, 128), 128)].T
        col = o + lax.broadcasted_iota(jnp.int32, (128, 128), 1)
        slab_ref[:, o:o + 128] = jnp.where(col <= row, block, 0.0)


def factor_and_solve(a, proj, basis):
    vm = pl.BlockSpec(memory_space=pltpu.VMEM)
    n = a.shape[0]
    return pl.pallas_call(
        diag_kernel,
        out_shape=(jax.ShapeDtypeStruct((2, n, 128), f32), jax.ShapeDtypeStruct((128, n), f32)),
        in_specs=[vm] * 3,
        out_specs=[vm] * 2,
        scratch_shapes=[pltpu.VMEM(a.shape, f32), pltpu.VMEM((n, 128), f32)],
        compiler_params=pltpu.CompilerParams(vmem_limit_bytes=48 * 2**20),
        name="diag",
    )(a, proj, basis)


def shards(panel, row_k, mask, a_low, a_diag, sketch):
    basis, proj, full = sketch_sums(panel, row_k, mask, a_low, a_diag, sketch)
    n = basis.shape[0]
    return factor_and_solve(full.reshape(n, n), proj, basis)


def solution(mesh):
    return jax.shard_map(
        shards,
        mesh=mesh,
        in_specs=(
            P("rows", "cols", None, None),
            P("cols", "rows", None),
            P("rows", "cols"),
            P("rows", None, None),
            P("rows", None),
            P(),
        ),
        out_specs=(P("rows", None, None), P("rows", None)),
        check_vma=False,
    )
```

time: 253 us -> 157 us (0.62)
  Pallas kernels: 42.9 us -> 148 us
  blocking collectives: 62.4 us -> 0 us
  waiting for transfers between devices: 60.9 us -> 0 us
  starting transfers between devices: 32.4 us -> 0 us
  local copies, waits for them, and re-layouts: 22.6 us -> 7.71 us
  matrix products: 14.2 us -> 0 us
  between operations: 14.4 us -> 0.67 us
    pallas_call x2, Pallas kernels: 42.9 us -> 148 us  [the longest x1 111 us: sketch_sums(): pl.pallas_call(functools.partial(sketch_kernel, NC=NC, NR=NR), out_shape=...]
    all_to_all x5 -> x0, blocking collectives: 62.4 us -> none  [the longest x3 37.5 us: from_everyone(): lax.all_to_all(jnp.broadcast_to(value[None], (count, *value.shape)), axis...]
    all_to_all x6 -> x0, waiting for transfers between devices: 60.9 us -> none  [the longest x3 38.6 us: from_everyone(): lax.all_to_all(jnp.broadcast_to(value[None], (count, *value.shape)), axis...]
    all_to_all x6 -> x0, starting transfers between devices: 32.3 us -> none  [the longest x3 16.7 us: from_everyone(): lax.all_to_all(jnp.broadcast_to(value[None], (count, *value.shape)), axis...]
    dot_general x13 -> x0, matrix products: 14.2 us -> none  [the longest x3 3.64 us: low_term(): jnp.einsum('ibr,irp->bip', outer, inner_core, preferred_element_type=f32)]
    convert_element_type x9 -> x0, local copies, waits for them, and re-layouts: 6.31 us -> none  [the longest x5 5.03 us: total_of(): return whole[:len(lines)].reshape(value.shape).astype(jnp.float32)]
    another operation x4 -> x0, local copies, waits for them, and re-layouts: 4.51 us -> none  [the longest x2 4.03 us: split_up(): return jnp.moveaxis(value.reshape(*before, count, -1, *after), dim, 0)]
    unnamed x14 -> x13, local copies, waits for them, and re-layouts: 4.09 us -> 7.71 us
  transfers between devices with their start and end apart: 7 -> 0, of which waited for: 6 -> 0; matrix products, arithmetic and copies ran while one was open for 12% -> 0% of each run, Pallas kernels for 2% -> 0%
where the time goes in v2:
time: 157 us
  Pallas kernels  148 us (94%)
  local copies, waits for them, and re-layouts  7.71 us (5%)
    pallas_call x1, Pallas kernels, sketch_sums(): pl.pallas_call(functools.partial(sketch_kernel, NC=NC, NR=NR), out_shape=...  111 us
    pallas_call x1, Pallas kernels, factor_and_solve(): pl.pallas_call(diag_kernel, out_shape=(jax.ShapeDtypeStruct((2, n, 128),...  37.7 us
    unnamed x13, local copies, waits for them, and re-layouts  7.71 us

profile of v2, /device:TPU:1, one launch (start us, length us, event | category | flops | bytes accessed | tf_op | source)
XLA Modules:
  0.0 156.8 jit_solution(6004063001061028846)
XLA Ops:
  0.6 1.1 copy.8.sketch
  1.7 0.0 copy-start.1
  1.7 1.4 copy-done.1
  3.1 0.0 copy-start.2
  3.1 1.0 copy-done.2
  4.2 0.0 copy-start.3
  4.2 1.0 copy-done.3
  5.2 0.0 copy-start.4
  5.2 0.9 copy-done.4
  6.1 0.0 copy-start.5
  6.1 0.7 copy-done.5
  6.8 110.8 %sketches.1 = (f32[1024,128]{1,0:T(8,128)S(1)}, bf16[1024,128]{1,0:T(8,128)(2,1)S(1)}, bf16[8,4,2,16,1024]{4,3,2,1,0:T(8,128)(2,1)}) custom-call(bf16[2,3,1024,128]{3,2,1,0:T(8,128)(2,1)S(1)} %copy-done.1, bf16[3,128,128]{2,1,0:T(8,128)(2,1)S(1)} %copy-done.4, s32[2,3]{1,0:T(2,128)S(1)} %copy-done.5, bf16[2,1024,128]{2,1,0:T(8,128)(2,1)S(1)} %copy-done.2, ...), custom_call_target="tpu_custom_call" | custom-call | tf_op jit(solution)/shard_map/sketches/pallas_call | solution.py:387
  117.6 0.0 copy-start
  117.6 1.6 %copy-done = bf16[8,4,2,16,1024]{4,3,2,1,0:T(8,128)(2,1)S(1)} copy-done((bf16[8,4,2,16,1024]{4,3,2,1,0:T(8,128)(2,1)S(1)}, bf16[8,4,2,16,1024]{4,3,2,1,0:T(8,128)(2,1)}, u32[]{:S(2)}) %copy-start) | copy-done | bytes 2097176
  119.2 37.7 %diag.1 = (f32[2,1024,128]{2,1,0:T(8,128)}, f32[128,1024]{1,0:T(8,128)}) custom-call(bf16[1024,1024]{1,0:T(8,128)(2,1)S(1)} %bitcast.1, bf16[1024,128]{1,0:T(8,128)(2,1)S(1)} %get-tuple-element.6.proj_ref, f32[1024,128]{1,0:T(8,128)S(1)} %get-tuple-element.7.basis_ref), custom_call_target="tpu_custom_call" | custom-call | tf_op jit(solution)/shard_map/diag/pallas_call | solution.py:455
Async XLA Ops:
  1.7 1.4 copy-start.1
  3.1 1.0 copy-start.2
  4.2 1.0 copy-start.3
  5.2 0.9 copy-start.4
  6.1 0.7 copy-start.5
  117.6 1.6 %copy-start = (bf16[8,4,2,16,1024]{4,3,2,1,0:T(8,128)(2,1)S(1)}, bf16[8,4,2,16,1024]{4,3,2,1,0:T(8,128)(2,1)}, u32[]{:S(2)}) copy-start(bf16[8,4,2,16,1024]{4,3,2,1,0:T(8,128)(2,1)} %get-tuple-element.5) | copy-start | bytes 6291460

commit v3 on v2

v3 whole, which is shorter than its diff:
```python
import functools

import jax
import jax.numpy as jnp
from jax import lax
from jax.experimental import pallas as pl
from jax.experimental.pallas import tpu as pltpu
from jax.sharding import PartitionSpec as P

f32 = jnp.float32
bf16 = jnp.bfloat16
MESH = pl.DeviceIdType.MESH
HIGHEST = lax.Precision.HIGHEST

def rcp(p):
    r = pl.reciprocal(p, approx=True)
    return r * (2.0 - p * r)

def strip_eliminate(parts, k0, s):
    first = parts[0]
    lanes = first.shape[1]
    row = lax.broadcasted_iota(jnp.int32, (s, lanes), 0)
    C = [jnp.broadcast_to(first[:, k0 + j:k0 + j + 1], (s, lanes)) for j in range(s)]
    parts = list(parts)
    diag = jnp.ones((s, lanes), f32)
    for j in range(s):
        p = C[j][j:j + 1, :]
        diag = jnp.where(row == j, p, diag)
        if j == s - 1: break
        M = jnp.where(row > j, C[j] * rcp(p), 0.0)
        for k in range(j + 1, s):
            C[k] = C[k] - M * C[k][j:j + 1, :]
        parts = [x - M * x[j:j + 1, :] for x in parts]
    R = lax.rsqrt(diag)
    return [x * R for x in parts]

def tn(a, b, prec=None):
    return lax.dot_general(a, b, (((0,), (0,)), ((), ())), preferred_element_type=f32, precision=prec)

def chol_block(D, n, s):
    eye = (lax.broadcasted_iota(jnp.int32, (n, n), 0) == lax.broadcasted_iota(jnp.int32, (n, n), 1)).astype(f32)
    WA, WE = D, eye
    outU, outE = [], []
    for k0 in range(0, n, s):
        a, e = strip_eliminate([WA[:s], WE[:s]], k0, s)
        outU.append(a)
        outE.append(e)
        if k0 + s < n:
            ab = a.astype(bf16)
            eb = e.astype(bf16)
            lhs = ab[:, k0 + s:]
            WA = WA[s:] - tn(lhs, ab)
            WE = WE[s:] - tn(lhs, eb)
            yield
    U = jnp.concatenate(outU, 0)
    E = jnp.concatenate(outE, 0)
    i0 = lax.broadcasted_iota(jnp.int32, (n, n), 0)
    i1 = lax.broadcasted_iota(jnp.int32, (n, n), 1)
    return jnp.where(i1 >= i0, U, 0.0), E


def together(*works):
    given = [None] * len(works)
    live = list(range(len(works)))
    while live:
        for n in list(live):
            try:
                next(works[n])
            except StopIteration as stop:
                given[n] = stop.value
                live.remove(n)
    return given


def inverse_pair(gram):
    n, s = 64, 16
    low = lax.broadcasted_iota(jnp.int32, (s, 128), 1) < n
    row = lax.broadcasted_iota(jnp.int32, (s, 128), 0)
    lanes = lax.broadcasted_iota(jnp.int32, (n, 128), 1)
    left = lanes < n
    A = jnp.where(left, gram[:n], gram[n:])
    E = (lax.rem(lanes, n) == lax.broadcasted_iota(jnp.int32, (n, 128), 0)).astype(f32)
    done = []
    for k0 in range(0, n, s):
        a, e = A[:s], E[:s]
        C = [
            jnp.where(
                low,
                jnp.broadcast_to(a[:, k0 + j:k0 + j + 1], (s, 128)),
                jnp.broadcast_to(a[:, n + k0 + j:n + k0 + j + 1], (s, 128)),
            )
            for j in range(s)
        ]
        diag = jnp.ones((s, 128), f32)
        for j in range(s):
            p = C[j][j:j + 1, :]
            diag = jnp.where(row == j, p, diag)
            if j == s - 1:
                break
            r = rcp(p)
            r = r * (2.0 - p * r)
            M = jnp.where(row > j, C[j] * r, 0.0)
            for k in range(j + 1, s):
                C[k] = C[k] - M * C[k][j:j + 1, :]
            a = a - M * a[j:j + 1, :]
            e = e - M * e[j:j + 1, :]
        R = lax.rsqrt(diag)
        a, e = a * R, e * R
        done.append(e)
        if k0 + s < n:
            both = tn(a, jnp.concatenate([a, e], axis=1), HIGHEST)
            both = [both[:, :128], both[:, 128:]]
            keep = left[k0 + s:]
            step = [jnp.where(keep, x[k0 + s:n], x[n + k0 + s:]) for x in both]
            A, E = A[s:] - step[0], E[s:] - step[1]
            yield
    E = jnp.concatenate(done, axis=0)
    return jnp.concatenate([jnp.where(left, E, 0.0), jnp.where(left, 0.0, E)], axis=0)


def nn(a, b, prec=None):
    return jnp.dot(a, b, preferred_element_type=f32, precision=prec)


def nt(a, b, prec=None):
    return lax.dot_general(a, b, (((1,), (1,)), ((), ())), preferred_element_type=f32, precision=prec)


def low_lanes(n):
    return lax.broadcasted_iota(jnp.int32, (n, 128), 1) < 64


def panel_kernel(
    panel_in, row_in, mask, low_in, diag_in, sketch,
    panel_ref, slab_ref,
    panel, a_low, a_diag, ROW, LT, ACC, MIX, S2, DP, DRS, FULL, TS, XS, YS, RS, FB, SB, TH, PB, BS,
    A, LOW, INV, Y,
    lsem, zsend, zrecv, dsend, drecv, csend, crecv, xsend, xrecv, rsend, rrecv, asend, arecv, bsend, brecv,
    *, NC, NR,
):
    B = NR * 128
    share = B // NC
    half = NC // 2
    strips = 8
    wide = B // (NC // strips)
    c = lax.axis_index("cols")
    z = lax.axis_index("rows")
    core, chip = lax.rem(c, 2), lax.div(c, 2)
    other = {"cols": c + 1 - 2 * core}
    barrier = pltpu.get_barrier_semaphore()

    def col_of(d):
        return lax.rem(c + d, NC)

    def chip_of(d):
        return lax.rem(chip + d, half)

    def row_of(d):
        return lax.rem(z + d + NR, NR)

    def slab(owner):
        return pl.ds(pl.multiple_of(owner * 128, 128), 128)

    def each(n, body):
        def step(d, carry):
            body(d)
            return carry
        lax.fori_loop(1, n, step, 0)

    loads = [
        pltpu.make_async_copy(row_in, ROW.at[:, slab(z), :], lsem.at[0]),
        pltpu.make_async_copy(panel_in, panel, lsem.at[1]),
        pltpu.make_async_copy(low_in, a_low, lsem.at[2]),
        pltpu.make_async_copy(diag_in, a_diag, lsem.at[3]),
    ]
    for load in loads:
        load.start()
    each(NC, lambda d: pl.semaphore_signal(barrier, 1, device_id={"cols": col_of(d)}, device_id_type=MESH))
    each(NR, lambda d: pl.semaphore_signal(barrier, 1, device_id={"rows": row_of(d)}, device_id_type=MESH))
    S2[...] = jnp.concatenate([sketch[...], sketch[...]], axis=1)
    for j in range(3):
        ACC[j] = jnp.zeros_like(ACC[j])
    loads[0].wait()
    pl.semaphore_wait(barrier, NC + NR - 2)

    def hop(way, step, j, owner):
        place = ROW.at[j, slab(owner), :]
        return pltpu.make_async_remote_copy(
            src_ref=place, dst_ref=place,
            send_sem=zsend.at[way, step, j], recv_sem=zrecv.at[way, step, j],
            device_id={"rows": row_of(1 if way == 0 else -1)}, device_id_type=MESH,
        )

    def absorb(owner, j):
        r = ROW[j, slab(owner), :]
        rt = r.T
        LT[640 + 128 * j:768 + 128 * j, slab(owner)] = rt
        right = jnp.concatenate(
            [panel[0, j, slab(owner), :], panel[1, j, slab(owner), :], r, S2[slab(owner), :]], axis=1
        )
        ACC[j] += nn(rt, right)

    last = NR // 2 - 1

    def passes(way, step, j):
        return step < last or (step == last and (way == 0) == (j < 2))

    hops = []
    for j in range(3):
        for way in range(2):
            if passes(way, 0, j):
                hops.append(hop(way, 0, j, z))
                hops[-1].start()
    loads[1].wait()
    for j in range(3):
        absorb(z, j)
    loads[2].wait()
    for i in range(2):
        LT[384 + 128 * i:512 + 128 * i, :] = a_low[i].T
    for s in range(last + 1):
        came = []
        for j in range(3):
            for way in range(2):
                if not passes(way, s, j):
                    continue
                owner = row_of(-1 - s if way == 0 else 1 + s)
                hop(way, s, j, owner).wait_recv()
                if passes(way, s + 1, j):
                    hops.append(hop(way, s + 1, j, owner))
                    hops[-1].start()
                came.append((owner, j))
        for owner, j in came:
            absorb(owner, j)

    part = jnp.zeros((128, B), f32)
    for j in range(3):
        square = pltpu.roll(ACC[j, 64:128, 256:384], 64, 1)
        square = jnp.where(low_lanes(64), square, 0.0).astype(bf16)
        square = jnp.concatenate([square, jnp.zeros((64, 128), bf16)], axis=0)
        own = nn(ROW[j, slab(z), :], square).astype(bf16)
        part = part + nn(own, LT[640 + 128 * j:768 + 128 * j, :])
    DP[...] = part.astype(bf16)

    def piece(owner):
        return (
            pl.ds(pl.multiple_of(lax.rem(owner, strips) * 16, 16), 16),
            pl.ds(pl.multiple_of(lax.div(owner, strips) * wide, 128), wide),
        )

    def send_diag(d):
        rows, columns = piece(col_of(d))
        pltpu.make_async_remote_copy(
            src_ref=DP.at[rows, columns], dst_ref=DRS.at[d - 1],
            send_sem=dsend.at[0], recv_sem=drecv.at[0],
            device_id={"cols": col_of(d)}, device_id_type=MESH,
        ).start()

    def all_in(ref, sem):
        pltpu.make_async_copy(ref, ref, sem).wait()

    each(NC, send_diag)

    weight = []
    for i in range(2):
        for j in range(3):
            block = ACC[j, :, 128 * i:128 * i + 128] * mask[i, j].astype(f32)
            flat = jnp.where(low_lanes(64), pltpu.roll(block[64:, :], 64, 1), 0.0).astype(bf16)
            m = 3 * i + j
            turned = block.T[64:, :]
            if m % 2 == 0:
                turned = jnp.where(low_lanes(64), pltpu.roll(turned, 64, 1), 0.0)
            else:
                turned = jnp.where(low_lanes(64), 0.0, turned)
            weight.append(jnp.concatenate([turned.astype(bf16), jnp.zeros((64, 128), bf16)], axis=0))
            LT[64 * m:64 * m + 64, :] = nt(flat, panel[i, j]).astype(bf16)
    for t in range(3):
        m, n = 2 * t, 2 * t + 1
        MIX[:, 128 * t:128 * t + 128] = (
            nn(panel[m // 3, m % 3], weight[m]) + nn(panel[n // 3, n % 3], weight[n])
        ).astype(bf16)

    def spread(inner):
        keep = low_lanes(192)
        zero = jnp.zeros_like(inner)
        return jnp.concatenate([jnp.where(keep, inner, zero), jnp.where(keep, zero, inner)], axis=0)

    def send_sum(n, terms):
        TS[n] = terms.reshape(half, 2, share, 128)
        copy = pltpu.make_async_remote_copy(
            src_ref=TS.at[n, :, 1 - core], dst_ref=XS.at[n], send_sem=xsend.at[n], recv_sem=xrecv.at[n],
            device_id=other, device_id_type=MESH,
        )
        copy.start()
        return copy

    def pass_sum(n, copy):
        copy.wait_recv()
        YS[n] = TS[n, :, core] + XS[n]

        def send(d):
            pltpu.make_async_remote_copy(
                src_ref=YS.at[n, chip_of(d)], dst_ref=RS.at[n, d - 1],
                send_sem=rsend.at[n], recv_sem=rrecv.at[n],
                device_id={"cols": col_of(2 * d)}, device_id_type=MESH,
            ).start()

        each(half, send)

    def end_sum(n):
        all_in(RS.at[n], rrecv.at[n])
        return YS[n, chip] + jnp.sum(RS[n], axis=0)

    def start_gather(n, whole, own):
        place = whole.at[chip, core]
        place[...] = own

        def send(d):
            pltpu.make_async_remote_copy(
                src_ref=place, dst_ref=place, send_sem=asend.at[n], recv_sem=arecv.at[n],
                device_id={"cols": col_of(2 * d)}, device_id_type=MESH,
            ).start()

        each(half, send)

    def end_gather(n, whole):
        all_in(whole.at[pl.ds(0, half - 1), core], arecv.at[n])
        place = whole.at[:, core]
        copy = pltpu.make_async_remote_copy(
            src_ref=place, dst_ref=place, send_sem=bsend.at[n], recv_sem=brecv.at[n],
            device_id=other, device_id_type=MESH,
        )
        copy.start()
        copy.wait_recv()
        return whole[...].reshape(B, 128)

    def low_share(inner, up):
        total = jnp.zeros((share, 128), f32)
        zero = jnp.zeros((64, 128), bf16)
        for i in range(2):
            half = inner[128 * i + 64:128 * i + 128] if up else inner[128 * i:128 * i + 64]
            keep = low_lanes(64) if i == 0 else jnp.logical_not(low_lanes(64))
            half = jnp.where(keep, half, 0.0).astype(bf16)
            right = jnp.concatenate([half, zero] if up else [zero, half], axis=0)
            total = total + nn(a_low[i, pl.ds(pl.multiple_of(c * share, share), share), :], right)
        return total

    def back_terms(back):
        zero = jnp.zeros((64, 128), bf16)
        total = jnp.zeros((B, 128), f32)
        for j in range(3):
            mine = jnp.where(low_lanes(64), back[64 * j:64 * j + 64], back[192 + 64 * j:256 + 64 * j])
            total = total + nn(ROW[j], jnp.concatenate([mine.astype(bf16), zero], axis=0))
        return total

    nb = B // 128
    strip = lax.rem(c, strips)
    pair = lax.div(strip, 2)
    early = min(2, nb)

    def to_chip(d, group):
        place = FULL.at[group, pair, core, :, columns]
        return pltpu.make_async_remote_copy(
            src_ref=place, dst_ref=place,
            send_sem=csend.at[GROUPS.index(group), d - 1], recv_sem=crecv.at[GROUPS.index(group), d - 1],
            device_id={"cols": col_of(2 * d)}, device_id_type=MESH,
        )

    GROUPS = [pl.ds(0, early)] + ([pl.ds(early, nb - early)] if nb > early else [])

    def to_core(group):
        place = FULL.at[group, :, core]
        return pltpu.make_async_remote_copy(
            src_ref=place, dst_ref=place,
            send_sem=dsend.at[2 + GROUPS.index(group)], recv_sem=drecv.at[2 + GROUPS.index(group)],
            device_id=other, device_id_type=MESH,
        )

    def pass_on(group):
        each(half, lambda d: to_chip(d, group).wait_recv())
        to_core(group).start()

    def block_step(kb):
        o = kb * 128
        rest = o + 128
        top = FULL[kb].reshape(128, B)[:, o:].astype(f32)
        if kb:
            top = top + A[o:rest, o:]
        U, E = yield from chol_block(top[:, :128], 128, 16)
        A[o:rest, o:rest] = U
        Eb = E.astype(bf16)
        INV[kb] = Eb
        if rest < B:
            across = nn(Eb, top[:, 128:].astype(bf16))
            A[o:rest, rest:] = across
            ab = across.astype(bf16)
            LOW[rest:, o:rest] = ab.T
            yield
            for ib in range(kb + 1, nb):
                r = ib * 128
                gone = nn(LOW[r:r + 128, o:rest], ab[:, r - rest:])
                A[r:r + 128, r:] = A[r:r + 128, r:] - gone if kb else -gone
        block = A[o:rest, slab(z)].T
        row = z * 128 + lax.broadcasted_iota(jnp.int32, (128, 128), 0)
        col = o + lax.broadcasted_iota(jnp.int32, (128, 128), 1)
        slab_ref[:, o:rest] = jnp.where(col <= row, block, 0.0)

    to_do = list(range(nb))

    def some_steps(n):
        for _ in range(n):
            if to_do:
                together(block_step(to_do.pop(0)))

    probe = jnp.concatenate([ACC[j, :64, 384:512] for j in range(3)], axis=0)
    x = send_sum(0, nn(MIX[...], spread(probe).astype(bf16)))
    low = low_share(nn(LT[384:640, :], S2[...]), True)
    pass_sum(0, x)
    loads[3].wait()
    all_in(DRS, drecv.at[0])
    rows, columns = piece(c)
    own = a_diag[rows, columns] - (
        DP[rows, columns].astype(f32) + jnp.sum(DRS[...].astype(f32), axis=0)
    )
    FULL[z, pair, core, :, columns] = own.astype(bf16)

    def send_rows(d):
        place = FULL.at[z, pair, core, :, columns]
        pltpu.make_async_remote_copy(
            src_ref=place, dst_ref=place, send_sem=dsend.at[1], recv_sem=drecv.at[1],
            device_id={"rows": row_of(d)}, device_id_type=MESH,
        ).start()

    each(NR, send_rows)
    start_gather(0, FB, (low - end_sum(0)).astype(bf16))
    all_in(FULL.at[pl.ds(0, NR - 1), pair, core, :, columns], drecv.at[1])
    each(half, lambda d: to_chip(d, GROUPS[0]).start())
    first = end_gather(0, FB)

    inner = nn(LT[:640, :], first)
    x = send_sum(1, back_terms(inner[:384]))
    low = low_share(inner[384:], False)
    pass_on(GROUPS[0])
    pass_sum(1, x)
    for group in GROUPS[1:]:
        each(half, lambda d: to_chip(d, group).start())
    to_core(GROUPS[0]).wait_recv()
    some_steps(1)
    start_gather(1, SB, (low - end_sum(1)).astype(bf16))
    some_steps(1)
    second = end_gather(1, SB)

    inner = nn(LT[384:, :], second)
    fore = jnp.concatenate([inner[256 + 128 * j:320 + 128 * j] for j in range(3)], axis=0)
    x = send_sum(2, nn(MIX[...], spread(fore).astype(bf16)))
    low = low_share(inner[:256], True)
    for group in GROUPS[1:]:
        pass_on(group)
    pass_sum(2, x)
    for group in GROUPS[1:]:
        to_core(group).wait_recv()
    some_steps(1)
    start_gather(2, TH, low - end_sum(2))
    some_steps(1)
    third = end_gather(2, TH)

    gram = nn(third.T, third, HIGHEST)
    if to_do:
        inverse, _ = together(inverse_pair(gram), block_step(to_do.pop(0)))
    else:
        inverse, = together(inverse_pair(gram))
    basis = nt(third, inverse, HIGHEST)
    BS[...] = basis

    inner = nn(LT[:640, :], basis.astype(bf16))
    x = send_sum(3, back_terms(inner[:384]))
    low = low_share(inner[384:], False)
    pass_sum(3, x)
    some_steps(1)
    start_gather(3, PB, (low - end_sum(3)).astype(bf16))
    some_steps(nb)
    Y[...] = end_gather(3, PB).astype(f32)

    left = low_lanes(128)
    for kb in range(nb):
        o = kb * 128
        y = nn(INV[kb], Y[o:o + 128, :].astype(bf16))
        if o + 128 < B:
            Y[o + 128:, :] -= nn(LOW[o + 128:, o:o + 128], y.astype(bf16))
        cols = BS[o:o + 128, :]
        panel_ref[0, o:o + 128, :] = jnp.where(left, cols, pltpu.roll(y, 64, 1))
        panel_ref[1, o:o + 128, :] = jnp.where(left, pltpu.roll(cols, 64, 1), y)

    for h in hops:
        h.wait_send()
    all_in(DRS, dsend.at[0])
    all_in(FULL.at[pl.ds(0, NR - 1), pair, core, :, columns], dsend.at[1])
    for group in GROUPS:
        each(half, lambda d: to_chip(d, group).wait_send())
        to_core(group).wait_send()
    for n, whole in enumerate((FB, SB, TH, PB)):
        all_in(XS.at[n], xsend.at[n])
        all_in(RS.at[n], rsend.at[n])
        all_in(whole.at[pl.ds(0, half - 1), core], asend.at[n])
        all_in(whole.at[:, core], bsend.at[n])


def shards(panel, row_k, mask, a_low, a_diag, sketch):
    NC, NR = lax.axis_size("cols"), lax.axis_size("rows")
    B = NR * 128
    share = B // NC
    half = NC // 2
    wide = B // (NC // 8)
    vm = pl.BlockSpec(memory_space=pltpu.VMEM)
    anywhere = pl.BlockSpec(memory_space=pl.ANY)
    dma = pltpu.SemaphoreType.DMA
    shape = jax.ShapeDtypeStruct
    return pl.pallas_call(
        functools.partial(panel_kernel, NC=NC, NR=NR),
        out_shape=(shape((2, B, 128), f32), shape((128, B), f32)),
        in_specs=[anywhere, anywhere, pl.BlockSpec(memory_space=pltpu.SMEM), anywhere, anywhere, vm],
        out_specs=[vm] * 2,
        scratch_shapes=[
            pltpu.VMEM((2, 3, B, 128), bf16),
            pltpu.VMEM((2, B, 128), bf16),
            pltpu.VMEM((128, B), f32),
            pltpu.VMEM((3, B, 128), bf16),
            pltpu.VMEM((1024, B), bf16),
            pltpu.VMEM((3, 128, 512), f32),
            pltpu.VMEM((B, 384), bf16),
            pltpu.VMEM((B, 128), bf16),
            pltpu.VMEM((128, B), bf16),
            pltpu.VMEM((NC - 1, 16, wide), bf16),
            pltpu.VMEM((NR, 4, 2, 16, B), bf16),
            pltpu.VMEM((4, half, 2, share, 128), f32),
            pltpu.VMEM((4, half, share, 128), f32),
            pltpu.VMEM((4, half, share, 128), f32),
            pltpu.VMEM((4, half - 1, share, 128), f32),
            pltpu.VMEM((half, 2, share, 128), bf16),
            pltpu.VMEM((half, 2, share, 128), bf16),
            pltpu.VMEM((half, 2, share, 128), f32),
            pltpu.VMEM((half, 2, share, 128), bf16),
            pltpu.VMEM((B, 128), f32),
            pltpu.VMEM((B, B), f32),
            pltpu.VMEM((B, B), bf16),
            pltpu.VMEM((NR, 128, 128), bf16),
            pltpu.VMEM((B, 128), f32),
            dma((4,)), dma((2, 4, 3)), dma((2, 4, 3)), dma((4,)), dma((4,)),
            dma((2, half)), dma((2, half)),
            dma((4,)), dma((4,)), dma((4,)), dma((4,)), dma((4,)), dma((4,)), dma((4,)), dma((4,)),
        ],
        compiler_params=pltpu.CompilerParams(
            collective_id=0, has_side_effects=True, vmem_limit_bytes=56 * 2**20
        ),
        name="panel",
    )(panel, row_k, mask, a_low, a_diag, sketch)


def solution(mesh):
    return jax.shard_map(
        shards,
        mesh=mesh,
        in_specs=(
            P("rows", "cols", None, None),
            P("cols", "rows", None),
            P("rows", "cols"),
            P("rows", None, None),
            P("rows", None),
            P(),
        ),
        out_specs=(P("rows", None, None), P("rows", None)),
        check_vma=False,
    )
```

time: 157 us -> 114 us (0.73)
  Pallas kernels: 148 us -> 109 us
  local copies, waits for them, and re-layouts: 7.71 us -> 4.86 us
    pallas_call x2 -> x1, Pallas kernels: 148 us -> 109 us  [shards(): pl.pallas_call(functools.partial(panel_kernel, NC=NC, NR=NR), out_shape=(...]
    unnamed x13 -> x5, local copies, waits for them, and re-layouts: 7.71 us -> 4.86 us
where the time goes in v3:
time: 114 us
  Pallas kernels  109 us (96%)
  local copies, waits for them, and re-layouts  4.86 us (4%)
    pallas_call x1, Pallas kernels, shards(): pl.pallas_call(functools.partial(panel_kernel, NC=NC, NR=NR), out_shape=(...  109 us
    unnamed x5, local copies, waits for them, and re-layouts  4.86 us

profile of v3, /device:TPU:1, one launch (start us, length us, event | category | flops | bytes accessed | tf_op | source)
XLA Modules:
  0.0 114.1 jit_solution(11598461652241804930)
XLA Ops:
  0.6 1.7 %copy.8.sketch = bf16[1024,64]{1,0:T(8,128)(2,1)} copy(bf16[1024,64]{0,1:T(8,128)(2,1)} %param.11) | data formatting | bytes 262144 | tf_op args[5]
  2.4 108.6 %panel.1 = (f32[2,1024,128]{2,1,0:T(8,128)}, f32[128,1024]{1,0:T(8,128)}) custom-call(bf16[2,3,1024,128]{3,2,1,0:T(8,128)(2,1)} %panel_in.1, bf16[3,128,128]{2,1,0:T(8,128)(2,1)} %row_in.1, s32[2,3]{1,0:T(2,128)} %mask.1, bf16[2,1024,128]{2,1,0:T(8,128)(2,1)} %low_in.1, f32[128,1024]{1,0:T(8,128)} %diag_in.1, bf16[1024,64]{1,0:T(8,128)(2,1)} %copy.8.sketch), custom_call_target="tpu_custom_call" | custom-call | tf_op jit(solution)/shard_map/panel/pallas_call | solution.py:517
  111.0 0.0 copy-start
  111.0 2.3 %copy.11 = f32[2,1024,128]{2,1,0:T(8,128)} copy(f32[2,1024,128]{2,1,0:T(8,128)} %get-tuple-element.4) | data formatting | bytes 2097152
  113.3 0.0 copy-done
  113.3 0.8 copy.12
Async XLA Ops:
  111.0 2.3 %copy-start = (f32[128,1024]{1,0:T(8,128)S(1)}, f32[128,1024]{1,0:T(8,128)}, u32[]{:S(2)}) copy-start(f32[128,1024]{1,0:T(8,128)} %get-tuple-element.5) | copy-start | bytes 1572868

commit v4 on v3

--- a/solution.py
+++ b/solution.py
@@ -133,7 +133,7 @@
 def panel_kernel(
     panel_in, row_in, mask, low_in, diag_in, sketch,
     panel_ref, slab_ref,
-    panel, a_low, a_diag, ROW, LT, ACC, MIX, S2, DP, DRS, FULL, TS, XS, YS, RS, FB, SB, TH, PB, BS,
+    panel, a_low, a_diag, ROW, LT, ACC, MIX, S2, DP, DX, DY, DRS, FULL, TS, XS, YS, RS, FB, SB, TH, PB, BS,
     A, LOW, INV, Y,
     lsem, zsend, zrecv, dsend, drecv, csend, crecv, xsend, xrecv, rsend, rrecv, asend, arecv, bsend, brecv,
     *, NC, NR,
@@ -146,6 +146,7 @@
     c = lax.axis_index("cols")
     z = lax.axis_index("rows")
     core, chip = lax.rem(c, 2), lax.div(c, 2)
+    mine = pl.ds(pl.multiple_of(c * share, share), share)
     other = {"cols": c + 1 - 2 * core}
     barrier = pltpu.get_barrier_semaphore()
 
@@ -175,13 +176,14 @@
     ]
     for load in loads:
         load.start()
-    each(NC, lambda d: pl.semaphore_signal(barrier, 1, device_id={"cols": col_of(d)}, device_id_type=MESH))
+    each(half, lambda d: pl.semaphore_signal(barrier, 1, device_id={"cols": col_of(2 * d)}, device_id_type=MESH))
+    pl.semaphore_signal(barrier, 1, device_id=other, device_id_type=MESH)
     each(NR, lambda d: pl.semaphore_signal(barrier, 1, device_id={"rows": row_of(d)}, device_id_type=MESH))
-    S2[...] = jnp.concatenate([sketch[...], sketch[...]], axis=1)
+    S2[...] = jnp.concatenate([sketch[...], sketch[...]], axis=0).T
     for j in range(3):
         ACC[j] = jnp.zeros_like(ACC[j])
     loads[0].wait()
-    pl.semaphore_wait(barrier, NC + NR - 2)
+    pl.semaphore_wait(barrier, half + NR - 1)
 
     def hop(way, step, j, owner):
         place = ROW.at[j, slab(owner), :]
@@ -239,26 +241,23 @@
         square = jnp.concatenate([square, jnp.zeros((64, 128), bf16)], axis=0)
         own = nn(ROW[j, slab(z), :], square).astype(bf16)
         part = part + nn(own, LT[640 + 128 * j:768 + 128 * j, :])
-    DP[...] = part.astype(bf16)
-
-    def piece(owner):
-        return (
-            pl.ds(pl.multiple_of(lax.rem(owner, strips) * 16, 16), 16),
-            pl.ds(pl.multiple_of(lax.div(owner, strips) * wide, 128), wide),
-        )
-
-    def send_diag(d):
-        rows, columns = piece(col_of(d))
-        pltpu.make_async_remote_copy(
-            src_ref=DP.at[rows, columns], dst_ref=DRS.at[d - 1],
-            send_sem=dsend.at[0], recv_sem=drecv.at[0],
-            device_id={"cols": col_of(d)}, device_id_type=MESH,
-        ).start()
+    DP[...] = part.astype(bf16).reshape(4, 2, 16, B)
 
     def all_in(ref, sem):
         pltpu.make_async_copy(ref, ref, sem).wait()
 
-    each(NC, send_diag)
+    diag_swap = pltpu.make_async_remote_copy(
+        src_ref=DP.at[:, 1 - core], dst_ref=DX, send_sem=dsend.at[0], recv_sem=drecv.at[0],
+        device_id=other, device_id_type=MESH,
+    )
+    diag_swap.start()
+
+    def place_of(owner):
+        pair = lax.rem(owner, 4)
+        return pair, lax.rem(pair + lax.div(owner, 4), NC // strips)
+
+    def columns_of(group):
+        return pl.ds(pl.multiple_of(group * wide, 128), wide)
 
     weight = []
     for i in range(2):
@@ -295,7 +294,7 @@
 
     def pass_sum(n, copy):
         copy.wait_recv()
-        YS[n] = TS[n, :, core] + XS[n]
+        YS[n] = (TS[n, :, core] + XS[n]).astype(bf16)
 
         def send(d):
             pltpu.make_async_remote_copy(
@@ -308,7 +307,7 @@
 
     def end_sum(n):
         all_in(RS.at[n], rrecv.at[n])
-        return YS[n, chip] + jnp.sum(RS[n], axis=0)
+        return TS[n, chip, core] + XS[n, chip] + jnp.sum(RS[n].astype(f32), axis=0)
 
     def start_gather(n, whole, own):
         place = whole.at[chip, core]
@@ -333,15 +332,15 @@
         copy.wait_recv()
         return whole[...].reshape(B, 128)
 
-    def low_share(inner, up):
-        total = jnp.zeros((share, 128), f32)
+    def low_rows(inner, up, rows):
+        total = jnp.zeros((rows.size, 128), f32)
         zero = jnp.zeros((64, 128), bf16)
         for i in range(2):
             half = inner[128 * i + 64:128 * i + 128] if up else inner[128 * i:128 * i + 64]
             keep = low_lanes(64) if i == 0 else jnp.logical_not(low_lanes(64))
             half = jnp.where(keep, half, 0.0).astype(bf16)
             right = jnp.concatenate([half, zero] if up else [zero, half], axis=0)
-            total = total + nn(a_low[i, pl.ds(pl.multiple_of(c * share, share), share), :], right)
+            total = total + nn(a_low[i, rows, :], right)
         return total
 
     def back_terms(back):
@@ -353,31 +352,39 @@
         return total
 
     nb = B // 128
-    strip = lax.rem(c, strips)
-    pair = lax.div(strip, 2)
-    early = min(2, nb)
-
-    def to_chip(d, group):
-        place = FULL.at[group, pair, core, :, columns]
+    pair, group = place_of(chip)
+    columns = columns_of(group)
+
+    def to_chip(d, k):
+        place = FULL.at[pl.ds(2 * k, 2), pair, core, :, columns]
         return pltpu.make_async_remote_copy(
-            src_ref=place, dst_ref=place,
-            send_sem=csend.at[GROUPS.index(group), d - 1], recv_sem=crecv.at[GROUPS.index(group), d - 1],
+            src_ref=place, dst_ref=place, send_sem=csend.at[k, d - 1], recv_sem=crecv.at[k, d - 1],
             device_id={"cols": col_of(2 * d)}, device_id_type=MESH,
         )
 
-    GROUPS = [pl.ds(0, early)] + ([pl.ds(early, nb - early)] if nb > early else [])
-
-    def to_core(group):
-        place = FULL.at[group, :, core]
+    def counts(owner, k):
+        return (place_of(owner)[1] + 1) * wide > 256 * k
+
+    def spread_group(k):
+        @pl.when(counts(chip, k))
+        def _():
+            each(half, lambda d: to_chip(d, k).start())
+
+    def to_core(k):
+        place = FULL.at[pl.ds(2 * k, 2), :, core, :, pl.ds(256 * k, B - 256 * k)]
         return pltpu.make_async_remote_copy(
-            src_ref=place, dst_ref=place,
-            send_sem=dsend.at[2 + GROUPS.index(group)], recv_sem=drecv.at[2 + GROUPS.index(group)],
+            src_ref=place, dst_ref=place, send_sem=dsend.at[3 + k], recv_sem=drecv.at[3 + k],
             device_id=other, device_id_type=MESH,
         )
 
-    def pass_on(group):
-        each(half, lambda d: to_chip(d, group).wait_recv())
-        to_core(group).start()
+    def pass_on(k):
+        def take(d):
+            @pl.when(counts(chip_of(half - d), k))
+            def _():
+                to_chip(d, k).wait_recv()
+
+        each(half, take)
+        to_core(k).start()
 
     def block_step(kb):
         o = kb * 128
@@ -411,39 +418,51 @@
             if to_do:
                 together(block_step(to_do.pop(0)))
 
+    diag_swap.wait_recv()
+    DY[...] = (DP[:, core].astype(f32) + DX[...].astype(f32)).astype(bf16)
+
+    def send_diag(d):
+        to_pair, to_group = place_of(chip_of(d))
+        pltpu.make_async_remote_copy(
+            src_ref=DY.at[to_pair, :, columns_of(to_group)], dst_ref=DRS.at[d - 1],
+            send_sem=dsend.at[1], recv_sem=drecv.at[1],
+            device_id={"cols": col_of(2 * d)}, device_id_type=MESH,
+        ).start()
+
     probe = jnp.concatenate([ACC[j, :64, 384:512] for j in range(3)], axis=0)
     x = send_sum(0, nn(MIX[...], spread(probe).astype(bf16)))
-    low = low_share(nn(LT[384:640, :], S2[...]), True)
+    low = low_rows(nn(LT[384:640, :], S2[...]), True, mine)
+    each(half, send_diag)
     pass_sum(0, x)
     loads[3].wait()
-    all_in(DRS, drecv.at[0])
-    rows, columns = piece(c)
+    all_in(DRS, drecv.at[1])
+    rows = pl.ds(pl.multiple_of((2 * pair + core) * 16, 16), 16)
     own = a_diag[rows, columns] - (
-        DP[rows, columns].astype(f32) + jnp.sum(DRS[...].astype(f32), axis=0)
+        DY[pair, :, columns].astype(f32) + jnp.sum(DRS[...].astype(f32), axis=0)
     )
     FULL[z, pair, core, :, columns] = own.astype(bf16)
 
     def send_rows(d):
         place = FULL.at[z, pair, core, :, columns]
         pltpu.make_async_remote_copy(
-            src_ref=place, dst_ref=place, send_sem=dsend.at[1], recv_sem=drecv.at[1],
+            src_ref=place, dst_ref=place, send_sem=dsend.at[2], recv_sem=drecv.at[2],
             device_id={"rows": row_of(d)}, device_id_type=MESH,
         ).start()
 
     each(NR, send_rows)
     start_gather(0, FB, (low - end_sum(0)).astype(bf16))
-    all_in(FULL.at[pl.ds(0, NR - 1), pair, core, :, columns], drecv.at[1])
-    each(half, lambda d: to_chip(d, GROUPS[0]).start())
+    all_in(FULL.at[pl.ds(0, NR - 1), pair, core, :, columns], drecv.at[2])
+    spread_group(0)
     first = end_gather(0, FB)
 
     inner = nn(LT[:640, :], first)
     x = send_sum(1, back_terms(inner[:384]))
-    low = low_share(inner[384:], False)
-    pass_on(GROUPS[0])
+    low = low_rows(inner[384:], False, mine)
+    pass_on(0)
     pass_sum(1, x)
-    for group in GROUPS[1:]:
-        each(half, lambda d: to_chip(d, group).start())
-    to_core(GROUPS[0]).wait_recv()
+    for k in range(1, nb // 2):
+        spread_group(k)
+    to_core(0).wait_recv()
     some_steps(1)
     start_gather(1, SB, (low - end_sum(1)).astype(bf16))
     some_steps(1)
@@ -452,16 +471,18 @@
     inner = nn(LT[384:, :], second)
     fore = jnp.concatenate([inner[256 + 128 * j:320 + 128 * j] for j in range(3)], axis=0)
     x = send_sum(2, nn(MIX[...], spread(fore).astype(bf16)))
-    low = low_share(inner[:256], True)
-    for group in GROUPS[1:]:
-        pass_on(group)
+    pass_on(1)
     pass_sum(2, x)
-    for group in GROUPS[1:]:
-        to_core(group).wait_recv()
+    low = low_rows(inner[:256], True, pl.ds(0, B))
+    to_core(1).wait_recv()
     some_steps(1)
-    start_gather(2, TH, low - end_sum(2))
+    start_gather(2, TH, end_sum(2).astype(bf16))
+    for k in range(2, nb // 2):
+        pass_on(k)
     some_steps(1)
-    third = end_gather(2, TH)
+    third = low - end_gather(2, TH).astype(f32)
+    for k in range(2, nb // 2):
+        to_core(k).wait_recv()
 
     gram = nn(third.T, third, HIGHEST)
     if to_do:
@@ -473,7 +494,7 @@
 
     inner = nn(LT[:640, :], basis.astype(bf16))
     x = send_sum(3, back_terms(inner[:384]))
-    low = low_share(inner[384:], False)
+    low = low_rows(inner[384:], False, mine)
     pass_sum(3, x)
     some_steps(1)
     start_gather(3, PB, (low - end_sum(3)).astype(bf16))
@@ -492,16 +513,48 @@
 
     for h in hops:
         h.wait_send()
-    all_in(DRS, dsend.at[0])
-    all_in(FULL.at[pl.ds(0, NR - 1), pair, core, :, columns], dsend.at[1])
-    for group in GROUPS:
-        each(half, lambda d: to_chip(d, group).wait_send())
-        to_core(group).wait_send()
+    diag_swap.wait_send()
+    all_in(DRS, dsend.at[1])
+    all_in(FULL.at[pl.ds(0, NR - 1), pair, core, :, columns], dsend.at[2])
+    for k in range(nb // 2):
+        @pl.when(counts(chip, k))
+        def _():
+            each(half, lambda d: to_chip(d, k).wait_send())
+        to_core(k).wait_send()
     for n, whole in enumerate((FB, SB, TH, PB)):
         all_in(XS.at[n], xsend.at[n])
         all_in(RS.at[n], rsend.at[n])
         all_in(whole.at[pl.ds(0, half - 1), core], asend.at[n])
         all_in(whole.at[:, core], bsend.at[n])
+
+
+def out_kernel(panel_in, slab_in, panel_out, slab_out, sems):
+    size = slab_in.shape[1] // 4
+    copies = []
+    for n in range(4):
+        cut = pl.ds(size * n, size)
+        for i in range(2):
+            copies.append((panel_in.at[i, cut], panel_out.at[i, cut]))
+        cut = pl.ds(32 * n, 32)
+        copies.append((slab_in.at[cut], slab_out.at[cut]))
+    copies = [pltpu.make_async_copy(a, b, sems.at[n]) for n, (a, b) in enumerate(copies)]
+    for copy in copies:
+        copy.start()
+    for copy in copies:
+        copy.wait()
+
+
+def written(panel_out, slab):
+    anywhere = pl.BlockSpec(memory_space=pl.ANY)
+    return pl.pallas_call(
+        out_kernel,
+        out_shape=(jax.ShapeDtypeStruct(panel_out.shape, f32), jax.ShapeDtypeStruct(slab.shape, f32)),
+        in_specs=[anywhere] * 2,
+        out_specs=[anywhere] * 2,
+        scratch_shapes=[pltpu.SemaphoreType.DMA((12,))],
+        compiler_params=pltpu.CompilerParams(vmem_limit_bytes=60 * 2**20),
+        name="written",
+    )(panel_out, slab)
 
 
 def shards(panel, row_k, mask, a_low, a_diag, sketch):
@@ -514,7 +567,7 @@
     anywhere = pl.BlockSpec(memory_space=pl.ANY)
     dma = pltpu.SemaphoreType.DMA
     shape = jax.ShapeDtypeStruct
-    return pl.pallas_call(
+    outs = pl.pallas_call(
         functools.partial(panel_kernel, NC=NC, NR=NR),
         out_shape=(shape((2, B, 128), f32), shape((128, B), f32)),
         in_specs=[anywhere, anywhere, pl.BlockSpec(memory_space=pltpu.SMEM), anywhere, anywhere, vm],
@@ -528,31 +581,34 @@
             pltpu.VMEM((3, 128, 512), f32),
             pltpu.VMEM((B, 384), bf16),
             pltpu.VMEM((B, 128), bf16),
-            pltpu.VMEM((128, B), bf16),
-            pltpu.VMEM((NC - 1, 16, wide), bf16),
+            pltpu.VMEM((4, 2, 16, B), bf16),
+            pltpu.VMEM((4, 16, B), bf16),
+            pltpu.VMEM((4, 16, B), bf16),
+            pltpu.VMEM((half - 1, 16, wide), bf16),
             pltpu.VMEM((NR, 4, 2, 16, B), bf16),
             pltpu.VMEM((4, half, 2, share, 128), f32),
             pltpu.VMEM((4, half, share, 128), f32),
-            pltpu.VMEM((4, half, share, 128), f32),
-            pltpu.VMEM((4, half - 1, share, 128), f32),
+            pltpu.VMEM((4, half, share, 128), bf16),
+            pltpu.VMEM((4, half - 1, share, 128), bf16),
             pltpu.VMEM((half, 2, share, 128), bf16),
             pltpu.VMEM((half, 2, share, 128), bf16),
-            pltpu.VMEM((half, 2, share, 128), f32),
+            pltpu.VMEM((half, 2, share, 128), bf16),
             pltpu.VMEM((half, 2, share, 128), bf16),
             pltpu.VMEM((B, 128), f32),
             pltpu.VMEM((B, B), f32),
             pltpu.VMEM((B, B), bf16),
             pltpu.VMEM((NR, 128, 128), bf16),
             pltpu.VMEM((B, 128), f32),
-            dma((4,)), dma((2, 4, 3)), dma((2, 4, 3)), dma((4,)), dma((4,)),
-            dma((2, half)), dma((2, half)),
+            dma((4,)), dma((2, 4, 3)), dma((2, 4, 3)), dma((3 + NR // 2,)), dma((3 + NR // 2,)),
+            dma((NR // 2, half)), dma((NR // 2, half)),
             dma((4,)), dma((4,)), dma((4,)), dma((4,)), dma((4,)), dma((4,)), dma((4,)), dma((4,)),
         ],
         compiler_params=pltpu.CompilerParams(
             collective_id=0, has_side_effects=True, vmem_limit_bytes=56 * 2**20
         ),
         name="panel",
-    )(panel, row_k, mask, a_low, a_diag, sketch)
+    )(panel, row_k, mask, a_low, a_diag, sketch.T)
+    return written(*outs)
 
 
 def solution(mesh):

time: 114 us -> 154 us (1.35)
  Pallas kernels: 109 us -> 153 us
  local copies, waits for them, and re-layouts: 4.86 us -> 0 us
    pallas_call x0 -> x1, Pallas kernels: none -> 48.9 us  [written(): pl.pallas_call(out_kernel, out_shape=(jax.ShapeDtypeStruct(panel_out.shap...]
    pallas_call x1, Pallas kernels: 109 us -> 104 us  [shards(): pl.pallas_call(functools.partial(panel_kernel, NC=NC, NR=NR), out_shape=(...]
    unnamed x5 -> x0, local copies, waits for them, and re-layouts: 4.86 us -> none
where the time goes in v4:
time: 154 us; the launch traced here: 153 us
  Pallas kernels  153 us (99%)
    pallas_call x1, Pallas kernels, shards(): pl.pallas_call(functools.partial(panel_kernel, NC=NC, NR=NR), out_shape=(...  104 us
    pallas_call x1, Pallas kernels, written(): pl.pallas_call(out_kernel, out_shape=(jax.ShapeDtypeStruct(panel_out.shap...  48.9 us

profile of v4, /device:TPU:1, one launch (start us, length us, event | category | flops | bytes accessed | tf_op | source)
XLA Modules:
  0.0 153.4 jit_solution(8008777883294201250)
XLA Ops:
  0.6 103.7 %panel.1 = (f32[2,1024,128]{2,1,0:T(8,128)}, f32[128,1024]{1,0:T(8,128)}) custom-call(bf16[2,3,1024,128]{3,2,1,0:T(8,128)(2,1)} %panel_in.1, bf16[3,128,128]{2,1,0:T(8,128)(2,1)} %row_in.1, s32[2,3]{1,0:T(2,128)} %mask.1, bf16[2,1024,128]{2,1,0:T(8,128)(2,1)} %low_in.1, f32[128,1024]{1,0:T(8,128)} %diag_in.1, bf16[64,1024]{1,0:T(8,128)(2,1)} %bitcast.1), custom_call_target="tpu_custom_call" | custom-call | tf_op jit(solution)/shard_map/panel/pallas_call | solution.py:570
  104.3 48.9 %written.1 = (f32[2,1024,128]{2,1,0:T(8,128)}, f32[128,1024]{1,0:T(8,128)}) custom-call(f32[2,1024,128]{2,1,0:T(8,128)} %get-tuple-element.4.panel_in, f32[128,1024]{1,0:T(8,128)} %get-tuple-element.5.slab_in), custom_call_target="tpu_custom_call" | custom-call | tf_op jit(solution)/shard_map/written/pallas_call | solution.py:549

commit v5 on v4

--- a/solution.py
+++ b/solution.py
@@ -23,16 +23,31 @@
     C = [jnp.broadcast_to(first[:, k0 + j:k0 + j + 1], (s, lanes)) for j in range(s)]
     parts = list(parts)
     diag = jnp.ones((s, lanes), f32)
+
+    def spread(x, n):
+        return jnp.broadcast_to(x[n:n + 1, :], (8, lanes))
+
+    def tall(x):
+        return jnp.concatenate([x] * (s // 8), axis=0)
+
+    p = spread(C[0], 0)
     for j in range(s):
-        p = C[j][j:j + 1, :]
-        diag = jnp.where(row == j, p, diag)
-        if j == s - 1: break
-        M = jnp.where(row > j, C[j] * rcp(p), 0.0)
+        diag = jnp.where(row == j, tall(p), diag)
+        if j == s - 1:
+            break
+        below = jnp.where(row > j, C[j], 0.0)
+        w = spread(C[j], j + 1) * spread(C[j + 1], j)
+        q = spread(C[j + 1], j + 1)
+        r = pl.reciprocal(p, approx=True)
+        u = 2.0 - p * r
+        p = q - (w * r) * u
+        M = (below * tall(r)) * tall(u)
         for k in range(j + 1, s):
             C[k] = C[k] - M * C[k][j:j + 1, :]
         parts = [x - M * x[j:j + 1, :] for x in parts]
     R = lax.rsqrt(diag)
     return [x * R for x in parts]
+
 
 def tn(a, b, prec=None):
     return lax.dot_general(a, b, (((0,), (0,)), ((), ())), preferred_element_type=f32, precision=prec)
@@ -219,8 +234,8 @@
     loads[2].wait()
     for i in range(2):
         LT[384 + 128 * i:512 + 128 * i, :] = a_low[i].T
+    came = []
     for s in range(last + 1):
-        came = []
         for j in range(3):
             for way in range(2):
                 if not passes(way, s, j):
@@ -230,9 +245,10 @@
                 if passes(way, s + 1, j):
                     hops.append(hop(way, s + 1, j, owner))
                     hops[-1].start()
+                if came:
+                    absorb(*came.pop())
                 came.append((owner, j))
-        for owner, j in came:
-            absorb(owner, j)
+    absorb(*came.pop())
 
     part = jnp.zeros((128, B), f32)
     for j in range(3):
@@ -528,31 +544,20 @@
         all_in(whole.at[:, core], bsend.at[n])
 
 
-def out_kernel(panel_in, slab_in, panel_out, slab_out, sems):
-    size = slab_in.shape[1] // 4
-    copies = []
-    for n in range(4):
-        cut = pl.ds(size * n, size)
-        for i in range(2):
-            copies.append((panel_in.at[i, cut], panel_out.at[i, cut]))
-        cut = pl.ds(32 * n, 32)
-        copies.append((slab_in.at[cut], slab_out.at[cut]))
-    copies = [pltpu.make_async_copy(a, b, sems.at[n]) for n, (a, b) in enumerate(copies)]
-    for copy in copies:
-        copy.start()
-    for copy in copies:
-        copy.wait()
+def out_kernel(panel_in, slab_in, panel_out, slab_out):
+    panel_out[...] = panel_in[...]
+    slab_out[...] = slab_in[...]
 
 
 def written(panel_out, slab):
-    anywhere = pl.BlockSpec(memory_space=pl.ANY)
+    n = panel_out.shape[1] // 4
+    blocks = [pl.BlockSpec((2, n, 128), lambda i: (0, i, 0)), pl.BlockSpec((32, slab.shape[1]), lambda i: (i, 0))]
     return pl.pallas_call(
         out_kernel,
+        grid=(4,),
         out_shape=(jax.ShapeDtypeStruct(panel_out.shape, f32), jax.ShapeDtypeStruct(slab.shape, f32)),
-        in_specs=[anywhere] * 2,
-        out_specs=[anywhere] * 2,
-        scratch_shapes=[pltpu.SemaphoreType.DMA((12,))],
-        compiler_params=pltpu.CompilerParams(vmem_limit_bytes=60 * 2**20),
+        in_specs=blocks,
+        out_specs=blocks,
         name="written",
     )(panel_out, slab)
 

time: 154 us -> 106 us (0.69)
  Pallas kernels: 153 us -> 105 us
    pallas_call x1, Pallas kernels: 48.9 us -> 3.55 us  [written(): pl.pallas_call(out_kernel, grid=(4,), out_shape=(jax.ShapeDtypeStruct(pan...]
    pallas_call x1, Pallas kernels: 104 us -> 102 us  [shards(): pl.pallas_call(functools.partial(panel_kernel, NC=NC, NR=NR), out_shape=(...]
where the time goes in v5:
time: 106 us
  Pallas kernels  105 us (99%)
    pallas_call x1, Pallas kernels, shards(): pl.pallas_call(functools.partial(panel_kernel, NC=NC, NR=NR), out_shape=(...  102 us
    pallas_call x1, Pallas kernels, written(): pl.pallas_call(out_kernel, grid=(4,), out_shape=(jax.ShapeDtypeStruct(pan...  3.55 us

profile of v5, /device:TPU:1, one launch (start us, length us, event | category | flops | bytes accessed | tf_op | source)
XLA Modules:
  0.0 106.1 jit_solution(8236389590476819373)
XLA Ops:
  0.6 101.9 %panel.1 = (f32[2,1024,128]{2,1,0:T(8,128)}, f32[128,1024]{1,0:T(8,128)}) custom-call(bf16[2,3,1024,128]{3,2,1,0:T(8,128)(2,1)} %panel_in.1, bf16[3,128,128]{2,1,0:T(8,128)(2,1)} %row_in.1, s32[2,3]{1,0:T(2,128)} %mask.1, bf16[2,1024,128]{2,1,0:T(8,128)(2,1)} %low_in.1, f32[128,1024]{1,0:T(8,128)} %diag_in.1, bf16[64,1024]{1,0:T(8,128)(2,1)} %bitcast.1), custom_call_target="tpu_custom_call" | custom-call | tf_op jit(solution)/shard_map/panel/pallas_call | solution.py:575
  102.5 3.5 %written.1 = (f32[2,1024,128]{2,1,0:T(8,128)}, f32[128,1024]{1,0:T(8,128)}) custom-call(f32[2,1024,128]{2,1,0:T(8,128)} %get-tuple-element.4.panel_in, f32[128,1024]{1,0:T(8,128)} %get-tuple-element.5.slab_in), custom_call_target="tpu_custom_call" | custom-call | tf_op jit(solution)/shard_map/written/pallas_call | solution.py:555

commit v6 on v5

--- a/solution.py
+++ b/solution.py
@@ -147,10 +147,10 @@
 
 def panel_kernel(
     panel_in, row_in, mask, low_in, diag_in, sketch,
-    panel_ref, slab_ref,
-    panel, a_low, a_diag, ROW, LT, ACC, MIX, S2, DP, DX, DY, DRS, FULL, TS, XS, YS, RS, FB, SB, TH, PB, BS,
+    panel_out, slab_out,
+    panel_ref, slab_ref, panel, a_low, a_diag, ROW, LT, ACC, MIX, S2, DP, DX, DY, DRS, FULL, TS, XS, YS, RS, FB, SB, TH, PB, BS,
     A, LOW, INV, Y,
-    lsem, zsend, zrecv, dsend, drecv, csend, crecv, xsend, xrecv, rsend, rrecv, asend, arecv, bsend, brecv,
+    lsem, osem, zsend, zrecv, dsend, drecv, csend, crecv, xsend, xrecv, rsend, rrecv, asend, arecv, bsend, brecv,
     *, NC, NR,
 ):
     B = NR * 128
@@ -474,8 +474,8 @@
     inner = nn(LT[:640, :], first)
     x = send_sum(1, back_terms(inner[:384]))
     low = low_rows(inner[384:], False, mine)
+    pass_sum(1, x)
     pass_on(0)
-    pass_sum(1, x)
     for k in range(1, nb // 2):
         spread_group(k)
     to_core(0).wait_recv()
@@ -487,8 +487,8 @@
     inner = nn(LT[384:, :], second)
     fore = jnp.concatenate([inner[256 + 128 * j:320 + 128 * j] for j in range(3)], axis=0)
     x = send_sum(2, nn(MIX[...], spread(fore).astype(bf16)))
+    pass_sum(2, x)
     pass_on(1)
-    pass_sum(2, x)
     low = low_rows(inner[:256], True, pl.ds(0, B))
     to_core(1).wait_recv()
     some_steps(1)
@@ -515,6 +515,8 @@
     some_steps(1)
     start_gather(3, PB, (low - end_sum(3)).astype(bf16))
     some_steps(nb)
+    leaving = [pltpu.make_async_copy(slab_ref, slab_out, osem.at[nb])]
+    leaving[0].start()
     Y[...] = end_gather(3, PB).astype(f32)
 
     left = low_lanes(128)
@@ -526,7 +528,12 @@
         cols = BS[o:o + 128, :]
         panel_ref[0, o:o + 128, :] = jnp.where(left, cols, pltpu.roll(y, 64, 1))
         panel_ref[1, o:o + 128, :] = jnp.where(left, pltpu.roll(cols, 64, 1), y)
-
+        made = pl.ds(o, 128)
+        leaving.append(pltpu.make_async_copy(panel_ref.at[:, made], panel_out.at[:, made], osem.at[kb]))
+        leaving[-1].start()
+
+    for copy in leaving:
+        copy.wait()
     for h in hops:
         h.wait_send()
     diag_swap.wait_send()
@@ -544,20 +551,38 @@
         all_in(whole.at[:, core], bsend.at[n])
 
 
-def out_kernel(panel_in, slab_in, panel_out, slab_out):
-    panel_out[...] = panel_in[...]
-    slab_out[...] = slab_in[...]
+def out_kernel(panel_in, slab_in, panel_out, slab_out, panel_here, slab_here, into, out):
+    parts = []
+    size = panel_in.shape[1] // 4
+    for n in range(4):
+        cut = pl.ds(size * n, size)
+        for i in range(2):
+            parts.append([ref.at[i, cut] for ref in (panel_in, panel_here, panel_out)])
+        cut = pl.ds(32 * n, 32)
+        parts.append([ref.at[cut] for ref in (slab_in, slab_here, slab_out)])
+    loads = [pltpu.make_async_copy(a, b, into.at[n]) for n, (a, b, _) in enumerate(parts)]
+    stores = [pltpu.make_async_copy(b, c, out.at[n]) for n, (_, b, c) in enumerate(parts)]
+    for copy in loads:
+        copy.start()
+    for load, store in zip(loads, stores):
+        load.wait()
+        store.start()
+    for copy in stores:
+        copy.wait()
 
 
 def written(panel_out, slab):
-    n = panel_out.shape[1] // 4
-    blocks = [pl.BlockSpec((2, n, 128), lambda i: (0, i, 0)), pl.BlockSpec((32, slab.shape[1]), lambda i: (i, 0))]
+    anywhere = pl.BlockSpec(memory_space=pl.ANY)
     return pl.pallas_call(
         out_kernel,
-        grid=(4,),
         out_shape=(jax.ShapeDtypeStruct(panel_out.shape, f32), jax.ShapeDtypeStruct(slab.shape, f32)),
-        in_specs=blocks,
-        out_specs=blocks,
+        in_specs=[anywhere] * 2,
+        out_specs=[anywhere] * 2,
+        scratch_shapes=[
+            pltpu.VMEM(panel_out.shape, f32), pltpu.VMEM(slab.shape, f32),
+            pltpu.SemaphoreType.DMA((12,)), pltpu.SemaphoreType.DMA((12,)),
+        ],
+        compiler_params=pltpu.CompilerParams(vmem_limit_bytes=60 * 2**20),
         name="written",
     )(panel_out, slab)
 
@@ -576,8 +601,10 @@
         functools.partial(panel_kernel, NC=NC, NR=NR),
         out_shape=(shape((2, B, 128), f32), shape((128, B), f32)),
         in_specs=[anywhere, anywhere, pl.BlockSpec(memory_space=pltpu.SMEM), anywhere, anywhere, vm],
-        out_specs=[vm] * 2,
+        out_specs=[anywhere] * 2,
         scratch_shapes=[
+            pltpu.VMEM((2, B, 128), f32),
+            pltpu.VMEM((128, B), f32),
             pltpu.VMEM((2, 3, B, 128), bf16),
             pltpu.VMEM((2, B, 128), bf16),
             pltpu.VMEM((128, B), f32),
@@ -604,7 +631,7 @@
             pltpu.VMEM((B, B), bf16),
             pltpu.VMEM((NR, 128, 128), bf16),
             pltpu.VMEM((B, 128), f32),
-            dma((4,)), dma((2, 4, 3)), dma((2, 4, 3)), dma((3 + NR // 2,)), dma((3 + NR // 2,)),
+            dma((4,)), dma((NR + 1,)), dma((2, 4, 3)), dma((2, 4, 3)), dma((3 + NR // 2,)), dma((3 + NR // 2,)),
             dma((NR // 2, half)), dma((NR // 2, half)),
             dma((4,)), dma((4,)), dma((4,)), dma((4,)), dma((4,)), dma((4,)), dma((4,)), dma((4,)),
         ],

time: 106 us -> 105 us (level)
    pallas_call x1, Pallas kernels: 3.55 us -> 2.33 us  [written(): pl.pallas_call(out_kernel, out_shape=(jax.ShapeDtypeStruct(panel_out.shap...]
where the time goes in v6:
time: 105 us
  Pallas kernels  104 us (99%)
    pallas_call x1, Pallas kernels, shards(): pl.pallas_call(functools.partial(panel_kernel, NC=NC, NR=NR), out_shape=(...  102 us
    pallas_call x1, Pallas kernels, written(): pl.pallas_call(out_kernel, out_shape=(jax.ShapeDtypeStruct(panel_out.shap...  2.33 us

profile of v6, /device:TPU:1, one launch (start us, length us, event | category | flops | bytes accessed | tf_op | source)
XLA Modules:
  0.0 104.8 jit_solution(6360636308550652304)
XLA Ops:
  0.6 101.7 %panel.1 = (f32[2,1024,128]{2,1,0:T(8,128)}, f32[128,1024]{1,0:T(8,128)}) custom-call(bf16[2,3,1024,128]{3,2,1,0:T(8,128)(2,1)} %panel_in.1, bf16[3,128,128]{2,1,0:T(8,128)(2,1)} %row_in.1, s32[2,3]{1,0:T(2,128)} %mask.1, bf16[2,1024,128]{2,1,0:T(8,128)(2,1)} %low_in.1, f32[128,1024]{1,0:T(8,128)} %diag_in.1, bf16[64,1024]{1,0:T(8,128)(2,1)} %bitcast.1), custom_call_target="tpu_custom_call" | custom-call | tf_op jit(solution)/shard_map/panel/pallas_call | solution.py:600
  102.3 2.3 %written.1 = (f32[2,1024,128]{2,1,0:T(8,128)}, f32[128,1024]{1,0:T(8,128)}) custom-call(f32[2,1024,128]{2,1,0:T(8,128)} %get-tuple-element.4.panel_in, f32[128,1024]{1,0:T(8,128)} %get-tuple-element.5.slab_in), custom_call_target="tpu_custom_call" | custom-call | tf_op jit(solution)/shard_map/written/pallas_call | solution.py:576

commit v7 on v6

--- a/solution.py
+++ b/solution.py
@@ -337,7 +337,7 @@
 
         each(half, send)
 
-    def end_gather(n, whole):
+    def end_gather(n, whole, meanwhile=lambda: None):
         all_in(whole.at[pl.ds(0, half - 1), core], arecv.at[n])
         place = whole.at[:, core]
         copy = pltpu.make_async_remote_copy(
@@ -345,6 +345,7 @@
             device_id=other, device_id_type=MESH,
         )
         copy.start()
+        meanwhile()
         copy.wait_recv()
         return whole[...].reshape(B, 128)
 
@@ -427,12 +428,21 @@
         col = o + lax.broadcasted_iota(jnp.int32, (128, 128), 1)
         slab_ref[:, o:rest] = jnp.where(col <= row, block, 0.0)
 
-    to_do = list(range(nb))
-
-    def some_steps(n):
+    def all_steps():
+        for kb in range(nb):
+            yield from block_step(kb)
+            yield
+
+    work = all_steps()
+
+    def in_turns(n):
         for _ in range(n):
-            if to_do:
-                together(block_step(to_do.pop(0)))
+            next(work, None)
+            yield
+
+    def advance(n):
+        for _ in in_turns(n):
+            pass
 
     diag_swap.wait_recv()
     DY[...] = (DP[:, core].astype(f32) + DX[...].astype(f32)).astype(bf16)
@@ -479,10 +489,10 @@
     for k in range(1, nb // 2):
         spread_group(k)
     to_core(0).wait_recv()
-    some_steps(1)
+    advance(7)
     start_gather(1, SB, (low - end_sum(1)).astype(bf16))
-    some_steps(1)
-    second = end_gather(1, SB)
+    advance(9)
+    second = end_gather(1, SB, lambda: advance(2))
 
     inner = nn(LT[384:, :], second)
     fore = jnp.concatenate([inner[256 + 128 * j:320 + 128 * j] for j in range(3)], axis=0)
@@ -491,33 +501,31 @@
     pass_on(1)
     low = low_rows(inner[:256], True, pl.ds(0, B))
     to_core(1).wait_recv()
-    some_steps(1)
+    advance(9)
     start_gather(2, TH, end_sum(2).astype(bf16))
     for k in range(2, nb // 2):
         pass_on(k)
-    some_steps(1)
-    third = low - end_gather(2, TH).astype(f32)
+    advance(7)
+    third = low - end_gather(2, TH, lambda: advance(2)).astype(f32)
     for k in range(2, nb // 2):
         to_core(k).wait_recv()
 
     gram = nn(third.T, third, HIGHEST)
-    if to_do:
-        inverse, _ = together(inverse_pair(gram), block_step(to_do.pop(0)))
-    else:
-        inverse, = together(inverse_pair(gram))
+    inverse, _ = together(inverse_pair(gram), in_turns(9))
     basis = nt(third, inverse, HIGHEST)
     BS[...] = basis
 
     inner = nn(LT[:640, :], basis.astype(bf16))
     x = send_sum(3, back_terms(inner[:384]))
     low = low_rows(inner[384:], False, mine)
+    advance(2)
     pass_sum(3, x)
-    some_steps(1)
+    advance(9)
     start_gather(3, PB, (low - end_sum(3)).astype(bf16))
-    some_steps(nb)
+    advance(13)
+    Y[...] = end_gather(3, PB, lambda: advance(9 * nb)).astype(f32)
     leaving = [pltpu.make_async_copy(slab_ref, slab_out, osem.at[nb])]
     leaving[0].start()
-    Y[...] = end_gather(3, PB).astype(f32)
 
     left = low_lanes(128)
     for kb in range(nb):

time: 105 us -> 104 us (level)
  no operation moved by 1% of the time
where the time goes in v7:
time: 104 us
  Pallas kernels  103 us (99%)
    pallas_call x1, Pallas kernels, shards(): pl.pallas_call(functools.partial(panel_kernel, NC=NC, NR=NR), out_shape=(...  101 us
    pallas_call x1, Pallas kernels, written(): pl.pallas_call(out_kernel, out_shape=(jax.ShapeDtypeStruct(panel_out.shap...  2.33 us

profile of v7, /device:TPU:1, one launch (start us, length us, event | category | flops | bytes accessed | tf_op | source)
XLA Modules:
  0.0 104.0 jit_solution(8475584278642161902)
XLA Ops:
  0.6 100.8 %panel.1 = (f32[2,1024,128]{2,1,0:T(8,128)}, f32[128,1024]{1,0:T(8,128)}) custom-call(bf16[2,3,1024,128]{3,2,1,0:T(8,128)(2,1)} %panel_in.1, bf16[3,128,128]{2,1,0:T(8,128)(2,1)} %row_in.1, s32[2,3]{1,0:T(2,128)} %mask.1, bf16[2,1024,128]{2,1,0:T(8,128)(2,1)} %low_in.1, f32[128,1024]{1,0:T(8,128)} %diag_in.1, bf16[64,1024]{1,0:T(8,128)(2,1)} %bitcast.1), custom_call_target="tpu_custom_call" | custom-call | tf_op jit(solution)/shard_map/panel/pallas_call | solution.py:608
  101.5 2.3 %written.1 = (f32[2,1024,128]{2,1,0:T(8,128)}, f32[128,1024]{1,0:T(8,128)}) custom-call(f32[2,1024,128]{2,1,0:T(8,128)} %get-tuple-element.4.panel_in, f32[128,1024]{1,0:T(8,128)} %get-tuple-element.5.slab_in), custom_call_target="tpu_custom_call" | custom-call | tf_op jit(solution)/shard_map/written/pallas_call | solution.py:584
